TPU v7x, 256 devices: a whole 4x4x8 slice. The times are simulated.
256 devices in a mesh: fsdp: 32 (over y, x, core), tp: 8 (over z).
Axes of the slice: x: 4, y: 4, z: 8, core: 2. Of those that a mesh axis runs over, the one named last changes fastest.
Arguments:
- gradient: bfloat16 [2, 8192, 8192], P(None, 'fsdp', 'tp'), may hold values from -188 to 188
- momentum: float32 [2, 8192, 8192], P(None, 'fsdp', 'tp'), may hold values from -6 to 6
- right_basis: float32 [2, 512, 8192], P(None, 'fsdp', 'tp'), may hold values from -6 to 6
Outputs:
- update: bfloat16 [2, 8192, 8192], P(None, 'fsdp', 'tp')
- momentum_next: float32 [2, 8192, 8192], P(None, 'fsdp', 'tp')
- basis_next: float32 [2, 512, 8192], P(None, 'fsdp', 'tp')
All inputs are finite; a program needn't handle non-finite values.
Results may differ from a plain program's by a relative error of at most 0.001.
Values sent between devices are 32-bit elements; how exact they have to be, the bound alone decides.
A program may use at most 64 MiB of HBM per device.

v0:
```python
import math

import jax
import jax.numpy as jnp
from jax import lax
from jax.sharding import PartitionSpec as P

D = 8192
RANK = 512


momentum_decay = 0.8
epsilon_sq = 1e-06


def orthonormal(triangle, left_rows):

    def solve_one(factor, matrix):
        return jax.scipy.linalg.solve_triangular(factor, matrix.T, lower=True).T

    return jax.vmap(solve_one)(triangle, left_rows)


def gram_local(left_rows):
    return jnp.einsum(
        "mik,mil->mkl",
        left_rows,
        left_rows,
        precision=lax.Precision.HIGHEST,
        preferred_element_type=jnp.float32,
    )


def shards(gradient, momentum, right_basis):
    highest = lax.Precision.HIGHEST
    blended = momentum + gradient.astype(jnp.float32)
    partial_value = jnp.einsum(
        "mic,mkc->mik",
        blended,
        lax.all_gather(right_basis, "fsdp", axis=1, tiled=True),
        precision=highest,
        preferred_element_type=jnp.float32,
    )
    left_whole = lax.psum(partial_value, "tp")
    gram_sum = lax.psum(gram_local(left_whole), "fsdp")
    left_orth = orthonormal(jnp.linalg.cholesky(gram_sum), left_whole)
    right_own = jnp.transpose(
        lax.psum_scatter(
            jnp.einsum(
                "mik,mic->kmc",
                left_orth,
                blended,
                precision=highest,
                preferred_element_type=jnp.float32,
            ),
            "fsdp",
            scatter_dimension=0,
            tiled=True,
        ),
        (1, 0, 2),
    )
    square_own = lax.psum(jnp.sum(right_own * right_own, axis=2), "tp")
    inverse_own = lax.rsqrt(square_own / D + epsilon_sq)
    basis_next = right_own * inverse_own[:, :, None]
    right_full, inverse = (
        lax.all_gather(right_own, "fsdp", axis=1, tiled=True),
        lax.all_gather(inverse_own, "fsdp", axis=1, tiled=True),
    )
    feedback = jnp.einsum(
        "mik,mkc->mic", left_orth, right_full, precision=highest, preferred_element_type=jnp.float32
    )
    momentum_next = blended - (1.0 - momentum_decay) * feedback
    scaled_left = left_orth * inverse[:, None, :]
    direction = jnp.einsum(
        "mik,mkc->mic",
        scaled_left,
        right_full,
        precision=highest,
        preferred_element_type=jnp.float32,
    )
    update = (math.sqrt(D / RANK) * direction).astype(jnp.bfloat16)
    return (update, momentum_next, basis_next)


def solution(mesh):
    placed = (P(None, "fsdp", "tp"), P(None, "fsdp", "tp"), P(None, "fsdp", "tp"))
    return jax.shard_map(
        shards,
        mesh=mesh,
        in_specs=placed,
        out_specs=(P(None, "fsdp", "tp"), P(None, "fsdp", "tp"), P(None, "fsdp", "tp")),
        check_vma=False,
    )
```

profile of v0, /device:TPU:1, one launch (start us, length us, event | category | flops | bytes accessed | tf_op | source)
XLA Modules:
  0.0 757.1 jit_solution(10585862332683896060)
XLA Ops:
  7.2 0.7 all-gather.4.cloned.1.call-update
  7.9 58.0 %all-gather.4.cloned.1.call-done = f32[2,512,1024]{2,1,0:T(8,128)} async-done(((f32[2,16,1024]{2,1,0:T(8,128)}), f32[2,512,1024]{2,1,0:T(8,128)}) %all-gather.4.cloned.1.call-update) | async-done | bytes 4194320 | tf_op jit(solution)/shard_map/all_gather | solution.py:40
  65.9 7.9 %fusion.10 = f32[2,256,512]{2,1,0:T(8,128)} fusion(f32[2,512,1024]{2,1,0:T(8,128)} %all-gather.4.cloned.1.call-done, f32[2,256,1024]{2,1,0:T(8,128)} %param.4, bf16[2,256,1024]{2,1,0:T(8,128)(2,1)} %param.3), kind=kOutput, calls=%fused_computation.24 | convolution fusion | flops 3222274048 | bytes 8388608 | tf_op jit(solution)/shard_map/mic,mkc->mik/dot_general | solution.py:37
  73.9 71.0 %all-reduce.6.cloned.1.call-done = f32[2,256,512]{2,1,0:T(8,128)} async-done(((f32[2,256,512]{2,1,0:T(8,128)}), f32[2,256,512]{2,1,0:T(8,128)}) %all-reduce.6.cloned.1.call-update) | async-done | bytes 1048592 | tf_op jit(solution)/shard_map/psum | solution.py:44
  144.9 4.7 fusion.46
  150.0 0.8 iota_compare_fusion
  150.8 119.1 %all-reduce.8.cloned.1.call-done = f32[2,512,512]{1,2,0:T(8,128)} async-done(((f32[2,512,512]{1,2,0:T(8,128)}), f32[2,512,512]{1,2,0:T(8,128)}) %all-reduce.8.cloned.1.call-update) | async-done | bytes 2097168 | tf_op jit(solution)/shard_map/psum | solution.py:45
  269.8 3.0 copy.117
  272.8 2.1 fusion.4
  274.9 1.3 copy-done.9
  276.3 23.5 %custom-call.35 = f32[2,128,128]{2,1,0:T(8,128)S(1)} custom-call(f32[2,128,128]{2,1,0:T(8,128)S(1)} %cholesky.274), custom_call_target="Cholesky" | custom-call | tf_op jit(solution)/shard_map/jit(cholesky)/cholesky | solution.py:46
  299.8 19.7 %custom-call.36 = f32[2,1,128,128]{2,3,1,0:T(8,128)S(1)} custom-call(f32[2,1,128,128]{3,2,1,0:T(8,128)S(1)} %select_bitcast_fusion.2), custom_call_target="InvertDiagBlocksLowerTriangular" | custom-call | tf_op jit(solution)/shard_map/jit(cholesky)/cholesky | solution.py:46
  319.7 1.5 constant_dynamic-update-slice_fusion.3
  321.2 1.5 convolution_subtract_fusion
  322.7 23.5 %custom-call.37 = f32[2,128,128]{2,1,0:T(8,128)S(1)} custom-call(f32[2,128,128]{2,1,0:T(8,128)S(1)} %cholesky.278), custom_call_target="Cholesky" | custom-call | tf_op jit(solution)/shard_map/jit(cholesky)/cholesky | solution.py:46
  346.2 19.9 %custom-call.38 = f32[2,1,128,128]{2,3,1,0:T(8,128)S(1)} custom-call(f32[2,1,128,128]{3,2,1,0:T(8,128)S(1)} %get-tuple-element.45), custom_call_target="InvertDiagBlocksLowerTriangular" | custom-call | tf_op jit(solution)/shard_map/jit(cholesky)/cholesky | solution.py:46
  366.5 1.6 convolution_subtract_fusion.3
  368.1 23.5 %custom-call.39 = f32[2,128,128]{2,1,0:T(8,128)S(1)} custom-call(f32[2,128,128]{2,1,0:T(8,128)S(1)} %cholesky.283), custom_call_target="Cholesky" | custom-call | tf_op jit(solution)/shard_map/jit(cholesky)/cholesky | solution.py:46
  391.6 19.7 %custom-call.40 = f32[2,1,128,128]{2,3,1,0:T(8,128)S(1)} custom-call(f32[2,1,128,128]{3,2,1,0:T(8,128)S(1)} %get-tuple-element.43), custom_call_target="InvertDiagBlocksLowerTriangular" | custom-call | tf_op jit(solution)/shard_map/jit(cholesky)/cholesky | solution.py:46
  411.5 1.5 convolution_subtract_fusion.5
  413.1 23.9 %custom-call.41 = f32[2,128,128]{2,1,0:T(8,128)S(1)} custom-call(f32[2,128,128]{2,1,0:T(8,128)S(1)} %convolution_subtract_fusion.5), custom_call_target="Cholesky" | custom-call | tf_op jit(solution)/shard_map/jit(cholesky)/cholesky | solution.py:46
  437.3 2.8 select_select_fusion
  440.1 14.6 %while.1 = (s32[]{:T(128)}, f32[2,512,512]{2,1,0:T(8,128)}, s32[4,2]{0,1:T(2,128)S(1)}, f32[4,2,128,128]{3,2,0,1:T(8,128)}, s32[]{:T(128)}) while((s32[]{:T(128)}, f32[2,512,512]{2,1,0:T(8,128)}, s32[4,2]{0,1:T(2,128)S(1)}, f32[4,2,128,128]{3,2,0,1:T(8,128)}, s32[]{:T(128)}) %tuple.39), condition=%wide.while_cond, body=%wide.while_body.sunk | while | flops 2 | bytes 263777 | solution.py:19
  440.1 0.6 fusion.56
  440.7 3.0 bitcast_dynamic-update-slice_fusion.2
  443.8 0.6 fusion.56
  444.4 3.0 bitcast_dynamic-update-slice_fusion.2
  447.5 0.6 fusion.56
  448.1 3.0 bitcast_dynamic-update-slice_fusion.2
  451.1 0.6 fusion.56
  451.7 2.9 bitcast_dynamic-update-slice_fusion.2
  454.6 79.4 %custom-call.42 = f32[2,4,128,128]{2,3,1,0:T(8,128)S(1)} custom-call(f32[2,4,128,128]{3,2,1,0:T(8,128)} %bitcast.79), custom_call_target="InvertDiagBlocksLowerTriangular" | custom-call | tf_op jit(solution)/shard_map/vmap(jit(_solve_triangular))/triangular_solve | solution.py:19
  534.5 1.5 convolution_subtract_fusion.2
  536.5 2.2 convolution_subtract_fusion.1
  538.7 1.3 fusion.31
  540.0 2.5 convolution_subtract_fusion.4
  542.6 1.3 fusion.30
  543.9 8.4 %convolution_bitcast_fusion = f32[512,2,1024]{0,2,1:T(8,128)} fusion(f32[2,256,1024]{2,1,0:T(8,128)S(1)} %copy-done, bf16[2,256,1024]{2,1,0:T(8,128)(2,1)S(1)} %copy-done.5, f32[2,128,256]{2,1,0:T(8,128)S(1)} %fusion.30, f32[2,128,256]{2,1,0:T(8,128)S(1)} %fusion.31, f32[2,128,256]{2,1,0:T(8,128)S(1)} %fusion.33, f32[2,128,256]{2,1,0:T(8,128)S(1)} %fusion.26), kind=kOutput, calls=%fused_computation.6 | convolution fusion | flops 3223060480 | bytes 8388608 | tf_op jit(solution)/shard_map/mik,mic->kmc/dot_general | solution.py:49
  552.4 7.4 copy.137
  561.6 119.9 %all-reduce.10.cloned.1.call-done = f32[512,2,1024]{2,1,0:T(2,128)} async-done(((f32[512,2,1024]{2,1,0:T(2,128)}), f32[512,2,1024]{2,1,0:T(2,128)}) %all-reduce.10.cloned.1.call-update) | async-done | bytes 4194320
  681.5 1.6 multiply_reduce_fusion
  683.2 14.0 %psum.23 = f32[2,16]{0,1:T(8,128)S(1)} all-reduce(f32[2,16]{0,1:T(8,128)S(1)} %get-tuple-element.38), channel_id=1, replica_groups=mesh['fsdp'=32,'tp'=8] {'tp'}, use_global_device_ids=true, to_apply=%region_12.13 | all-reduce | flops 32 | bytes 256 | tf_op jit(solution)/shard_map/psum | solution.py:62
  697.1 1.0 broadcast_multiply_fusion
  698.2 0.7 copy.144
  699.0 28.8 %all-gather = f32[32,16,2]{1,2,0:T(2,128)S(1)} all-gather(f32[1,16,2]{1,2,0:T(2,128)S(1)} %bitcast.78), channel_id=1, replica_groups=mesh['fsdp'=32,'tp'=8] {'fsdp'}, dimensions={0}, use_global_device_ids=true | all-gather | bytes 4224 | tf_op jit(solution)/shard_map/all_gather | solution.py:67
  727.8 7.9 %all-gather.6.cloned.1.call-done = f32[2,512,1024]{2,0,1:T(2,128)} async-done(((f32[2,16,1024]{2,0,1:T(2,128)}), f32[2,512,1024]{2,0,1:T(2,128)}) %all-gather.6.cloned.1.call-update) | async-done | bytes 4194320 | tf_op jit(solution)/shard_map/all_gather | solution.py:66
  735.7 8.7 %multiply_subtract_fusion = f32[2,256,1024]{2,1,0:T(8,128)} fusion(f32[2,512,1024]{2,0,1:T(2,128)} %all-gather.6.cloned.1.call-done, f32[2,256,1024]{2,1,0:T(8,128)S(1)} %copy-done, bf16[2,256,1024]{2,1,0:T(8,128)(2,1)} %param.3, f32[2,128,256]{2,1,0:T(8,128)S(1)} %fusion.30, f32[2,128,256]{2,1,0:T(8,128)S(1)} %copy-done.8, ...), kind=kOutput, calls=%fused_computation.9 | convolution fusion | flops 3224109056 | bytes 10485760 | tf_op jit(solution)/shard_map/mik,mkc->mic/dot_general | solution.py:69
  744.4 5.9 multiply_convert_fusion
  (61 shorter events, 4.4 us)
Async XLA Ops:
  7.2 58.8 %all-gather.4.cloned.1.call-start = ((), (), s32[]{:S(2)}) async-start(), calls=%async_computation | async-start | bytes 4325376 | tf_op jit(solution)/shard_map/all_gather | solution.py:40
  7.9 137.0 %all-reduce.6.cloned.1.call-start = ((), (), s32[]{:S(2)}) async-start(), calls=%async_computation.1 | async-start | bytes 2097152 | tf_op jit(solution)/shard_map/psum | solution.py:44
  73.8 196.0 %all-reduce.8.cloned.1.call-start = ((), (), s32[]{:S(2)}) async-start(), calls=%async_computation.2 | async-start | bytes 4194304 | tf_op jit(solution)/shard_map/psum | solution.py:45
  149.7 531.9 %all-reduce.10.cloned.1.call-start = ((), (), s32[]{:S(2)}) async-start(), calls=%async_computation.4 | async-start | bytes 8388608
  269.8 3.0 copy-start.6
  274.9 1.3 copy-start.9
  437.3 96.8 %copy-start.2 = (f32[2,256,512]{2,1,0:T(8,128)S(1)}, f32[2,256,512]{2,1,0:T(8,128)}, u32[]{:S(2)}) copy-start(f32[2,256,512]{2,1,0:T(8,128)} %all-reduce.6.cloned.1.call-done) | copy-start | bytes 3145732
  534.1 2.0 copy-start.10
  536.5 7.4 copy-start.3
  536.5 7.5 copy-start
  536.5 7.5 copy-start.5
  540.0 3.9 copy-start.7
  559.7 0.7 copy-start.11
  559.7 176.0 %copy-start.4 = (f32[2,128,256]{2,1,0:T(8,128)S(1)}, f32[2,128,256]{2,1,0:T(8,128)}, u32[]{:S(2)}) copy-start(f32[2,128,256]{2,1,0:T(8,128)} %copy-done.3) | copy-start | bytes 786436
  559.7 176.0 %copy-start.8 = (f32[2,128,256]{2,1,0:T(8,128)S(1)}, f32[2,128,256]{2,1,0:T(8,128)}, u32[]{:S(2)}) copy-start(f32[2,128,256]{2,1,0:T(8,128)} %copy-done.7) | copy-start | bytes 786436
  559.8 176.0 %all-gather.6.cloned.1.call-start = ((), (), s32[]{:S(2)}) async-start(), calls=%async_computation.3 | async-start | bytes 4325376 | tf_op jit(solution)/shard_map/all_gather | solution.py:66
  735.7 8.7 %copy-start.1 = (f32[2,512,1024]{2,0,1:T(2,128)S(1)}, f32[2,512,1024]{2,0,1:T(2,128)}, u32[]{:S(2)}) copy-start(f32[2,512,1024]{2,0,1:T(2,128)} %all-gather.6.cloned.1.call-done) | copy-start | bytes 12582916
Sparse Core Ops, SparseCore 0:
  10.6 55.2 all-gather.3
  74.0 70.8 all-reduce.5
  149.8 119.9 all-reduce.7
  559.9 121.6 all-reduce.9
  684.5 51.1 all-gather.5
where the time goes:
time: 762 us; the launch traced here: 757 us
  waiting for transfers between devices  377 us (49%)
  other arithmetic  242 us (32%)
  matrix products  52.1 us (7%)
  blocking collectives  42.8 us (6%)
  local copies, waits for them, and re-layouts  28.7 us (4%)
  between operations  15 us (2%)
    another operation x16, other arithmetic, shards(): left_orth = orthonormal(jnp.linalg.cholesky(gram_sum), left_whole)  154 us
    unnamed x6, waiting for transfers between devices  121 us
    psum x1, waiting for transfers between devices, shards(): gram_sum = lax.psum(gram_local(left_whole), 'fsdp')  119 us
    another operation x4, other arithmetic, solve_one(): return jax.scipy.linalg.solve_triangular(factor, matrix.T, lower=True).T  83 us
    psum x1, waiting for transfers between devices, shards(): left_whole = lax.psum(partial_value, 'tp')  71 us
    all_gather x1, waiting for transfers between devices, shards(): lax.all_gather(right_basis, 'fsdp', axis=1, tiled=True)  58 us
    all_gather x1, blocking collectives, shards(): lax.all_gather(inverse_own, 'fsdp', axis=1, tiled=True)  28.8 us
  transfers between devices with their start and end apart: 5, of which 5 were waited for; matrix products, arithmetic and copies ran while one was open for 0% of the time, Pallas kernels for 0%

commit v1 on v0

v1 whole, which is shorter than its diff:
```python
import math

import jax
import jax.numpy as jnp
from jax import lax
from jax.experimental import pallas as pl
from jax.experimental.pallas import tpu as pltpu
from jax.sharding import PartitionSpec as P

D = 8192
RANK = 512
momentum_decay = 0.8
epsilon_sq = 1e-06
MESH = pl.DeviceIdType.MESH
F32 = jnp.float32
HIGH = lax.Precision.HIGH
HIGHEST = lax.Precision.HIGHEST
VMEM_BYTES = 56 * 1024 * 1024


def dot(a, b, ca, cb, precision):
    return lax.dot_general(
        a, b, (((ca,), (cb,)), ((), ())), precision=precision, preferred_element_type=F32
    )


class Place:
    def __init__(self, send_sem, recv_sem):
        f = lax.axis_index("fsdp")
        self.f = f
        self.z = lax.axis_index("tp")
        self.c = lax.rem(f, 2)
        self.x = lax.rem(f // 2, 4)
        self.y = f // 8
        self.send_sem, self.recv_sem = send_sem, recv_sem
        self.count = 0
        self.open = []

    def dev(self, y=None, x=None, z=None, c=None):
        y = self.y if y is None else y
        x = self.x if x is None else x
        c = self.c if c is None else c
        z = self.z if z is None else z
        return ((y * 4 + x) * 2 + c, z)

    def partner(self):
        return self.dev(c=1 - self.c)

    def xs(self, d):
        return lax.rem(self.x + d, 4)

    def ys(self, d):
        return lax.rem(self.y + d, 4)

    def zs(self, d):
        return lax.rem(self.z + d, 8)

    def copy(self, src, dst, to):
        i = self.count
        self.count += 1
        cp = pltpu.make_async_remote_copy(
            src_ref=src,
            dst_ref=dst,
            send_sem=self.send_sem.at[i],
            recv_sem=self.recv_sem.at[i],
            device_id=to,
            device_id_type=MESH,
        )
        cp.start()
        self.open.append(cp)
        return cp

    def barrier(self, peers):
        sem = pltpu.get_barrier_semaphore()
        for p in peers:
            pl.semaphore_signal(sem, inc=1, device_id=p, device_id_type=MESH)
        pl.semaphore_wait(sem, len(peers))

    def drain(self):
        for cp in self.open:
            cp.wait_send()
        self.open = []


def received(copies):
    for cp in copies:
        cp.wait_recv()


class Gather:
    def __init__(self, pc, buf):
        self.pc, self.buf = pc, buf

    def first(self):
        pc, buf = self.pc, self.buf
        self.one = []
        for d in (1, 3, 2):
            a, b = buf.at[pc.y, pc.x, 0], buf.at[pc.y, pc.x, 1]
            self.one.append(pc.copy(a, a, pc.dev(x=pc.xs(d))))
            self.one.append(pc.copy(b, b, pc.dev(y=pc.ys(d))))

    def second(self):
        pc, buf = self.pc, self.buf
        received(self.one)
        self.two = []
        for d in (1, 3, 2):
            a, b = buf.at[pc.y, :, 0], buf.at[:, pc.x, 1]
            self.two.append(pc.copy(a, a, pc.dev(y=pc.ys(d))))
            self.two.append(pc.copy(b, b, pc.dev(x=pc.xs(d))))

    def finish(self):
        received(self.two)


class Scatter:
    def __init__(self, pc, buf, r1, acc, r2):
        self.pc, self.buf, self.r1, self.acc, self.r2 = pc, buf, r1, acc, r2

    def first(self):
        pc, buf = self.pc, self.buf
        self.one = []
        for d in (1, 3, 2):
            self.one.append(pc.copy(buf.at[pc.ys(d), :, 0], self.r1.at[0, d - 1], pc.dev(y=pc.ys(d))))
            self.one.append(pc.copy(buf.at[:, pc.xs(d), 1], self.r1.at[1, d - 1], pc.dev(x=pc.xs(d))))

    def second(self):
        pc, buf, r1, acc = self.pc, self.buf, self.r1, self.acc
        received(self.one)
        acc[0] = buf[pc.y, :, 0] + r1[0, 0] + r1[0, 1] + r1[0, 2]
        acc[1] = buf[:, pc.x, 1] + r1[1, 0] + r1[1, 1] + r1[1, 2]
        self.two = []
        for d in (1, 3, 2):
            self.two.append(pc.copy(acc.at[0, pc.xs(d)], self.r2.at[0, d - 1], pc.dev(x=pc.xs(d))))
            self.two.append(pc.copy(acc.at[1, pc.ys(d)], self.r2.at[1, d - 1], pc.dev(y=pc.ys(d))))

    def finish(self):
        pc, acc, r2 = self.pc, self.acc, self.r2
        received(self.two)
        own0 = acc[0, pc.x] + r2[0, 0] + r2[0, 1] + r2[0, 2]
        own1 = acc[1, pc.y] + r2[1, 0] + r2[1, 1] + r2[1, 2]
        return own0, own1


def reduce_kernel(
    grad, mom, rb, g_out, w_out, left_out,
    blend, blend_send, basis, lpart, lrecv, left,
    gbuf, gr1, gacc, gr2, zbuf, gfull,
    wbuf, wr1, wacc, wr2, wall, left_all,
    send_sem, recv_sem, local_sem,
):
    pc = Place(send_sem, recv_sem)
    c, x, y, z = pc.c, pc.x, pc.y, pc.z
    peers = [pc.partner()]
    peers += [pc.dev(x=pc.xs(d)) for d in (1, 2, 3)]
    peers += [pc.dev(y=pc.ys(d)) for d in (1, 2, 3)]
    peers += [pc.dev(z=pc.zs(d)) for d in range(1, 8)]
    pc.barrier(peers)

    basis_swap = pc.copy(rb.at[1 - c], basis.at[y, x, c], pc.partner())
    basis[y, x, c] = rb[c]
    blend_send[...] = mom[1 - c] + grad[1 - c].astype(F32)
    blend_swap = pc.copy(blend_send, blend.at[c], pc.partner())
    blend[c] = mom[c] + grad[c].astype(F32)
    basis_swap.wait_recv()
    gather = Gather(pc, basis)
    gather.first()
    gather.second()
    blend_swap.wait_recv()
    gather.finish()

    for half in range(2):
        part = dot(blend[half], basis[...].reshape(RANK, 1024), 1, 1, HIGHEST)
        lpart[4 * half:4 * half + 4] = part.reshape(4, 64, RANK)
    sums = []
    for d in (4, 3, 5, 2, 6, 1, 7):
        sums.append(pc.copy(lpart.at[pc.zs(d)], lrecv.at[d - 1], pc.dev(z=pc.zs(d))))
    received(sums)
    own = lpart[z]
    for d in range(7):
        own = own + lrecv[d]
    left[z] = own
    lefts = []
    for d in (1, 7, 2, 6, 3, 5, 4):
        lefts.append(pc.copy(left.at[z], left.at[z], pc.dev(z=pc.zs(d))))

    blocks = []
    for i in range(4):
        row = dot(own[:, 128 * i:128 * i + 128], own[:, :128 * i + 128], 0, 0, HIGHEST)
        blocks += [row[:, 128 * j:128 * j + 128] for j in range(i + 1)]
    gbuf[...] = jnp.concatenate(blocks, axis=0).reshape(4, 4, 2, 40, 128)
    gscatter = Scatter(pc, gbuf, gr1, gacc, gr2)
    gscatter.first()
    gscatter.second()
    own0, own1 = gscatter.finish()
    zbuf[z, 0] = own0
    zbuf[z, 1] = own1
    zs = []
    for d in (4, 3, 5, 2, 6, 1, 7):
        zs.append(pc.copy(zbuf.at[z], zbuf.at[z], pc.dev(z=pc.zs(d))))
    received(zs)
    total = zbuf[0]
    for d in range(1, 8):
        total = total + zbuf[d]
    gfull[y, x] = total
    ggather = Gather(pc, gfull)
    ggather.first()
    ggather.second()
    ggather.finish()
    g_copy = pltpu.make_async_copy(gfull, g_out, local_sem.at[0])
    g_copy.start()

    received(lefts)
    left_all[c] = left[pl.ds(4 * c, 4)]
    left_swap = pc.copy(left.at[pl.ds(4 * (1 - c), 4)], left_all.at[c], pc.partner())
    for i in range(4):
        lt = left[:, :, 128 * i:128 * i + 128].reshape(RANK, 128)
        part = dot(lt, blend[...].reshape(512, 1024), 0, 0, HIGHEST)
        wbuf[i] = part.reshape(4, 2, 16, 1024)
    wscatter = Scatter(pc, wbuf, wr1, wacc, wr2)
    wscatter.first()
    wscatter.second()
    own0, own1 = wscatter.finish()
    wall[c, y, x, 0] = own0
    wall[c, y, x, 1] = own1
    wgather = Gather(pc, wall.at[c])
    wgather.first()
    wgather.second()
    wgather.finish()
    w_swap = pc.copy(wall.at[c], wall.at[c], pc.partner())
    left_swap.wait_recv()
    left_copy = pltpu.make_async_copy(left_all, left_out, local_sem.at[1])
    left_copy.start()
    w_swap.wait_recv()
    w_copy = pltpu.make_async_copy(wall, w_out, local_sem.at[2])
    w_copy.start()
    g_copy.wait()
    left_copy.wait()
    w_copy.wait()
    pc.drain()


def factor_block(load):
    groups = 16
    a = [load(r) for r in range(groups)]
    lane = lax.broadcasted_iota(jnp.int32, (8, 128), 1)
    sub = lax.broadcasted_iota(jnp.int32, (8, 128), 0)
    out = [None] * groups

    def column(v, j):
        return jnp.broadcast_to(v[:, j:j + 1], (8, 128))

    for q in range(32):
        r0, s0, j0 = q // 2, 4 * (q % 2), 4 * q
        rows = [jnp.broadcast_to(a[r0][s0 + s:s0 + s + 1, :], (8, 128)) for s in range(4)]
        p = {(s, t): column(rows[s], j0 + t) for s in range(4) for t in range(s, 4)}
        inside = (lane >= j0) & (lane < j0 + 4)
        v = [jnp.where(inside, jnp.where(lane == j0 + s, 1.0, 0.0), rows[s]) for s in range(4)]
        low, inv = {}, []
        for s in range(4):
            inv.append(1.0 / p[s, s])
            for t in range(s + 1, 4):
                low[t, s] = p[s, t] * inv[s]
            for u in range(s + 1, 4):
                for t in range(u, 4):
                    p[u, t] = p[u, t] - low[u, s] * p[s, t]
        for t in range(1, 4):
            for s in range(t):
                v[t] = v[t] - low[t, s] * v[s]
        w = [v[s] * inv[s] for s in range(4)]
        for s in (2, 1, 0):
            for t in range(s + 1, 4):
                w[s] = w[s] - low[t, s] * w[t]
        done = [v[s] * lax.rsqrt(p[s, s]) for s in range(4)]
        o = done[0]
        for s in range(1, 4):
            o = jnp.where(sub == s0 + s, done[s], o)
        out[r0] = o if s0 == 0 else jnp.where(sub < 4, out[r0], o)
        for r in range(r0 if s0 == 0 else r0 + 1, groups):
            cols = [column(a[r], j0 + t) for t in range(4)]
            new = jnp.where(inside, 0.0, a[r])
            for s in range(4):
                new = new - cols[s] * w[s]
            a[r] = new
    return out


def factor_kernel(g, linv, work, tri):
    flat = g[...].reshape(1280, 128)
    k = 0
    for i in range(4):
        for j in range(i + 1):
            work[j, 128 * i:128 * i + 128] = flat[128 * k:128 * k + 128]
            k += 1
    row = lax.broadcasted_iota(jnp.int32, (RANK, 128), 0)
    col = lax.broadcasted_iota(jnp.int32, (RANK, 128), 1)
    for j in range(4):
        linv[j] = jnp.where(row == col + 128 * j, 1.0, 0.0)

    def panel(k, carry):
        off = pl.multiple_of(k * 128, 128)
        rows = factor_block(lambda r: work[k, pl.ds(off + 8 * r, 8), :])
        for r in range(16):
            tri[8 * r:8 * r + 8, :] = rows[r]
        own = jnp.where(row[:128] >= col[:128], tri[...], 0.0)
        below = jnp.where(row >= off + 128, dot(work[k], own, 1, 1, HIGHEST), 0.0)
        tri[...] = own
        for j in range(4):
            step = dot(own, linv[j, pl.ds(off, 128), :], 1, 0, HIGHEST)
            linv[j, pl.ds(off, 128), :] = step
            linv[j] = linv[j] - dot(below, step, 1, 0, HIGHEST)
            work[j] = work[j] - dot(below, below[128 * j:128 * j + 128], 1, 1, HIGHEST)
        return carry

    lax.fori_loop(0, 4, panel, 0)


def finish_kernel(
    grad, mom, linv, w, left, update, momentum_next, basis_next,
    tri, right, orth, sums, squares, send_sem, recv_sem,
):
    pc = Place(send_sem, recv_sem)
    c, z = pc.c, pc.z
    pc.barrier([pc.partner()] + [pc.dev(z=pc.zs(d)) for d in range(1, 8)])
    swap = pc.copy(linv, tri.at[c], pc.partner())
    tri[c] = linv[...]

    def whole(m):
        return jnp.concatenate([tri[m, j] for j in range(4)], axis=1)

    def raw(m):
        t = whole(m)

        def part(j, carry):
            cols = pl.ds(pl.multiple_of(j * 256, 256), 256)
            wj = w[m, :, :, :, :, cols].reshape(RANK, 256)
            right[m, :, cols] = dot(t, wj, 1, 0, HIGH)
            return carry

        lax.fori_loop(0, 4, part, 0)
        r = right[m]
        sums[m] = dot(jnp.ones((8, 1024), F32), r * r, 1, 1, HIGHEST)

    raw(c)
    swap.wait_recv()
    raw(1 - c)
    pieces = [sums[m, 0:1, 128 * j:128 * j + 128] for m in range(2) for j in range(4)]
    squares[z] = jnp.concatenate(pieces, axis=0)
    zs = []
    for d in (4, 3, 5, 2, 6, 1, 7):
        zs.append(pc.copy(squares.at[z], squares.at[z], pc.dev(z=pc.zs(d))))
    for m in range(2):
        orth[m] = dot(left[m].reshape(256, RANK), whole(m), 1, 1, HIGH)

        def feed(j, carry, m=m):
            cols = pl.ds(pl.multiple_of(j * 256, 256), 256)
            back = dot(orth[m], right[m, :, cols], 1, 0, HIGH)
            blended = mom[m, :, cols] + grad[m, :, cols].astype(F32)
            momentum_next[m, :, cols] = blended - (1.0 - momentum_decay) * back
            return carry

        lax.fori_loop(0, 4, feed, 0)
    received(zs)
    total = squares[0]
    for d in range(1, 8):
        total = total + squares[d]
    inverse = lax.rsqrt(total / D + epsilon_sq)
    lane = lax.broadcasted_iota(jnp.int32, (16, RANK), 1)
    sub = lax.broadcasted_iota(jnp.int32, (16, RANK), 0)
    for m in range(2):
        inv = jnp.concatenate([inverse[4 * m + j:4 * m + j + 1] for j in range(4)], axis=1)
        orth[m] = orth[m] * inv
        pick = jnp.where(lane == pc.f * 16 + sub, inv, 0.0)

        def direction(j, carry, m=m, pick=pick):
            cols = pl.ds(pl.multiple_of(j * 256, 256), 256)
            rj = right[m, :, cols]
            out = math.sqrt(D / RANK) * dot(orth[m], rj, 1, 0, HIGH)
            update[m, :, cols] = out.astype(jnp.bfloat16)
            basis_next[m, :, cols] = dot(pick, rj, 1, 0, HIGHEST)
            return carry

        lax.fori_loop(0, 4, direction, 0)
    pc.drain()


def shards(gradient, momentum, right_basis):
    vmem = pl.BlockSpec(memory_space=pltpu.VMEM)
    anywhere = pl.BlockSpec(memory_space=pl.ANY)
    shape = lambda s: jax.ShapeDtypeStruct(s, F32)
    buf = lambda *s: pltpu.VMEM(s, F32)
    n1 = 85
    gram, w, left = pl.pallas_call(
        reduce_kernel,
        out_shape=(shape((4, 4, 2, 40, 128)), shape((2, 4, 4, 2, 16, 1024)), shape((2, 4, 64, RANK))),
        in_specs=[vmem] * 3,
        out_specs=[anywhere] * 3,
        scratch_shapes=[
            buf(2, 256, 1024), buf(256, 1024), buf(4, 4, 2, 16, 1024),
            buf(8, 64, RANK), buf(7, 64, RANK), buf(8, 64, RANK),
            buf(4, 4, 2, 40, 128), buf(2, 3, 4, 40, 128), buf(2, 4, 40, 128), buf(2, 3, 40, 128),
            buf(8, 2, 40, 128), buf(4, 4, 2, 40, 128),
            buf(4, 4, 2, 16, 1024), buf(2, 3, 4, 16, 1024), buf(2, 4, 16, 1024), buf(2, 3, 16, 1024),
            buf(2, 4, 4, 2, 16, 1024), buf(2, 4, 64, RANK),
            pltpu.SemaphoreType.DMA((n1,)), pltpu.SemaphoreType.DMA((n1,)), pltpu.SemaphoreType.DMA((3,)),
        ],
        compiler_params=pltpu.CompilerParams(
            collective_id=0, has_side_effects=True, vmem_limit_bytes=VMEM_BYTES
        ),
        name="reduce",
    )(gradient, momentum, right_basis)
    linv = pl.pallas_call(
        factor_kernel,
        out_shape=shape((4, RANK, 128)),
        in_specs=[vmem],
        out_specs=vmem,
        scratch_shapes=[buf(4, RANK, 128), buf(128, 128)],
        compiler_params=pltpu.CompilerParams(vmem_limit_bytes=VMEM_BYTES),
        name="factor",
    )(gram)
    n2 = 8
    return pl.pallas_call(
        finish_kernel,
        out_shape=(
            jax.ShapeDtypeStruct((2, 256, 1024), jnp.bfloat16), shape((2, 256, 1024)), shape((2, 16, 1024))
        ),
        in_specs=[vmem] * 5,
        out_specs=[vmem] * 3,
        scratch_shapes=[
            buf(2, 4, RANK, 128), buf(2, RANK, 1024), buf(2, 256, RANK), buf(2, 8, RANK), buf(8, 8, 128),
            pltpu.SemaphoreType.DMA((n2,)), pltpu.SemaphoreType.DMA((n2,)),
        ],
        compiler_params=pltpu.CompilerParams(
            collective_id=1, has_side_effects=True, vmem_limit_bytes=VMEM_BYTES
        ),
        name="finish",
    )(gradient, momentum, linv, w, left)


def solution(mesh):
    placed = (P(None, "fsdp", "tp"), P(None, "fsdp", "tp"), P(None, "fsdp", "tp"))
    return jax.shard_map(
        shards,
        mesh=mesh,
        in_specs=placed,
        out_specs=placed,
        check_vma=False,
    )
```

time: 762 us -> 219 us (0.29)
  waiting for transfers between devices: 377 us -> 0 us
  other arithmetic: 242 us -> 0 us
  Pallas kernels: 0 us -> 214 us
  matrix products: 52.1 us -> 0 us
  blocking collectives: 42.8 us -> 0 us
  local copies, waits for them, and re-layouts: 28.7 us -> 4.39 us
  between operations: 15 us -> 0.66 us
    another operation x20 -> x0, other arithmetic: 237 us -> none  [the longest x16 154 us: shards(): left_orth = orthonormal(jnp.linalg.cholesky(gram_sum), left_whole)]
    pallas_call x0 -> x3, Pallas kernels: none -> 214 us  [the longest x1 146 us: shards(): pl.pallas_call(reduce_kernel, out_shape=(shape((4, 4, 2, 40, 128)), shape...]
    psum x2 -> x0, waiting for transfers between devices: 190 us -> none  [the longest x1 119 us: shards(): gram_sum = lax.psum(gram_local(left_whole), 'fsdp')]
    unnamed x6 -> x0, waiting for transfers between devices: 121 us -> none
    all_gather x2 -> x0, waiting for transfers between devices: 65.9 us -> none  [the longest x1 58 us: shards(): lax.all_gather(right_basis, 'fsdp', axis=1, tiled=True)]
    dot_general x5 -> x0, matrix products: 35.6 us -> none  [the longest x1 8.69 us: shards(): jnp.einsum('mik,mkc->mic', left_orth, right_full, precision=highest, pref...]
    all_gather x1 -> x0, blocking collectives: 28.8 us -> none  [shards(): lax.all_gather(inverse_own, 'fsdp', axis=1, tiled=True)]
    another operation x13 -> x0, matrix products: 16.4 us -> none  [the longest x7 9.71 us: solve_one(): return jax.scipy.linalg.solve_triangular(factor, matrix.T, lower=True).T]
  transfers between devices with their start and end apart: 5 -> 0, of which waited for: 5 -> 0; matrix products, arithmetic and copies ran while one was open for 0% -> 0% of each run, Pallas kernels for 0% -> 0%
where the time goes in v1:
time: 219 us
  Pallas kernels  214 us (98%)
  local copies, waits for them, and re-layouts  4.39 us (2%)
    pallas_call x1, Pallas kernels, shards(): pl.pallas_call(reduce_kernel, out_shape=(shape((4, 4, 2, 40, 128)), shape...  146 us
    pallas_call x1, Pallas kernels, shards(): pl.pallas_call(factor_kernel, out_shape=shape((4, RANK, 128)), in_specs=[...  41.7 us
    pallas_call x1, Pallas kernels, shards(): pl.pallas_call(finish_kernel, out_shape=(jax.ShapeDtypeStruct((2, 256, 10...  26.6 us
    unnamed x7, local copies, waits for them, and re-layouts  4.39 us

profile of v1, /device:TPU:1, one launch (start us, length us, event | category | flops | bytes accessed | tf_op | source)
XLA Modules:
  0.0 219.3 jit_solution(12854417079893230422)
XLA Ops:
  0.6 145.9 %reduce.1 = (f32[4,4,2,40,128]{4,3,2,1,0:T(8,128)}, f32[2,4,4,2,16,1024]{5,4,3,2,1,0:T(8,128)}, f32[2,4,64,512]{3,2,1,0:T(8,128)}) custom-call(bf16[2,256,1024]{2,1,0:T(8,128)(2,1)} %grad.3, f32[2,256,1024]{2,1,0:T(8,128)} %mom.3, f32[2,16,1024]{2,1,0:T(8,128)} %rb.1), custom_call_target="tpu_custom_call" | custom-call | tf_op jit(solution)/shard_map/reduce/pallas_call | solution.py:392
  146.5 41.7 %factor.1.linv = f32[4,512,128]{2,1,0:T(8,128)} custom-call(f32[4,4,2,40,128]{4,3,2,1,0:T(8,128)} %get-tuple-element.6.g), custom_call_target="tpu_custom_call" | custom-call | tf_op jit(solution)/shard_map/factor/pallas_call | solution.py:411
  188.2 26.6 %finish.1 = (bf16[2,256,1024]{2,1,0:T(8,128)(2,1)}, f32[2,256,1024]{2,1,0:T(8,128)}, f32[2,16,1024]{2,1,0:T(8,128)}) custom-call(bf16[2,256,1024]{2,1,0:T(8,128)(2,1)} %grad.3, f32[2,256,1024]{2,1,0:T(8,128)} %mom.3, f32[4,512,128]{2,1,0:T(8,128)} %factor.1.linv, f32[2,4,4,2,16,1024]{5,4,3,2,1,0:T(8,128)} %get-tuple-element.7.w, ...), custom_call_target="tpu_custom_call" | custom-call | tf_op jit(solution)/shard_map/finish/pallas_call | solution.py:421
  214.9 0.0 copy-start
  214.9 2.4 %copy.9 = bf16[2,256,1024]{2,1,0:T(8,128)(2,1)} copy(bf16[2,256,1024]{2,1,0:T(8,128)(2,1)} %get-tuple-element.12) | data formatting | bytes 2097152
  217.3 0.0 copy-done
  217.3 0.0 copy-start.1
  217.3 1.3 copy.10
  218.6 0.0 copy-done.1
  218.6 0.7 copy.11
Async XLA Ops:
  214.9 2.4 %copy-start = (f32[2,256,1024]{2,1,0:T(8,128)S(1)}, f32[2,256,1024]{2,1,0:T(8,128)}, u32[]{:S(2)}) copy-start(f32[2,256,1024]{2,1,0:T(8,128)} %get-tuple-element.13) | copy-start | bytes 6291460
  217.3 1.3 copy-start.1

commit v2 on v1

v2 whole, which is shorter than its diff:
```python
import math

import jax
import jax.numpy as jnp
from jax import lax
from jax.experimental import pallas as pl
from jax.experimental.pallas import tpu as pltpu
from jax.sharding import PartitionSpec as P

D = 8192
RANK = 512
momentum_decay = 0.8
epsilon_sq = 1e-06
MESH = pl.DeviceIdType.MESH
F32 = jnp.float32
HIGH = lax.Precision.HIGH
HIGHEST = lax.Precision.HIGHEST
VMEM_BYTES = 56 * 1024 * 1024


def dot(a, b, ca, cb, precision):
    return lax.dot_general(
        a, b, (((ca,), (cb,)), ((), ())), precision=precision, preferred_element_type=F32
    )


class Place:
    def __init__(self, send_sem, recv_sem):
        f = lax.axis_index("fsdp")
        self.f = f
        self.z = lax.axis_index("tp")
        self.c = lax.rem(f, 2)
        self.x = lax.rem(f // 2, 4)
        self.y = f // 8
        self.send_sem, self.recv_sem = send_sem, recv_sem
        self.count = 0
        self.open = []

    def dev(self, y=None, x=None, z=None, c=None):
        y = self.y if y is None else y
        x = self.x if x is None else x
        c = self.c if c is None else c
        z = self.z if z is None else z
        return ((y * 4 + x) * 2 + c, z)

    def partner(self):
        return self.dev(c=1 - self.c)

    def xs(self, d):
        return lax.rem(self.x + d, 4)

    def ys(self, d):
        return lax.rem(self.y + d, 4)

    def zs(self, d):
        return lax.rem(self.z + d, 8)

    def copy(self, src, dst, to):
        i = self.count
        self.count += 1
        cp = pltpu.make_async_remote_copy(
            src_ref=src,
            dst_ref=dst,
            send_sem=self.send_sem.at[i],
            recv_sem=self.recv_sem.at[i],
            device_id=to,
            device_id_type=MESH,
        )
        cp.start()
        self.open.append(cp)
        return cp

    def barrier(self, peers):
        sem = pltpu.get_barrier_semaphore()
        for p in peers:
            pl.semaphore_signal(sem, inc=1, device_id=p, device_id_type=MESH)
        pl.semaphore_wait(sem, len(peers))

    def drain(self):
        for cp in self.open:
            cp.wait_send()
        self.open = []


def received(copies):
    for cp in copies:
        cp.wait_recv()


class Gather:
    def __init__(self, pc, buf):
        self.pc, self.buf = pc, buf

    def first(self):
        pc, buf = self.pc, self.buf
        self.one = []
        for d in (1, 3, 2):
            a, b = buf.at[pc.y, pc.x, 0], buf.at[pc.y, pc.x, 1]
            self.one.append(pc.copy(a, a, pc.dev(x=pc.xs(d))))
            self.one.append(pc.copy(b, b, pc.dev(y=pc.ys(d))))

    def second(self):
        pc, buf = self.pc, self.buf
        received(self.one)
        self.two = {}
        for d in (1, 3, 2):
            a, b = buf.at[pc.y, :, 0], buf.at[:, pc.x, 1]
            self.two[d] = (pc.copy(a, a, pc.dev(y=pc.ys(d))), pc.copy(b, b, pc.dev(x=pc.xs(d))))

    def finish(self):
        for d in (1, 3, 2):
            received(self.two[d])


class Scatter:
    def __init__(self, pc, buf, r1, acc, r2):
        self.pc, self.buf, self.r1, self.acc, self.r2 = pc, buf, r1, acc, r2

    def first(self):
        pc, buf = self.pc, self.buf
        self.one = []
        for d in (1, 3, 2):
            self.one.append(pc.copy(buf.at[pc.ys(d), :, 0], self.r1.at[0, d - 1], pc.dev(y=pc.ys(d))))
            self.one.append(pc.copy(buf.at[:, pc.xs(d), 1], self.r1.at[1, d - 1], pc.dev(x=pc.xs(d))))

    def second(self):
        pc, buf, r1, acc = self.pc, self.buf, self.r1, self.acc
        received(self.one)
        acc[0] = buf[pc.y, :, 0] + r1[0, 0] + r1[0, 1] + r1[0, 2]
        acc[1] = buf[:, pc.x, 1] + r1[1, 0] + r1[1, 1] + r1[1, 2]
        self.two = []
        for d in (1, 3, 2):
            self.two.append(pc.copy(acc.at[0, pc.xs(d)], self.r2.at[0, d - 1], pc.dev(x=pc.xs(d))))
            self.two.append(pc.copy(acc.at[1, pc.ys(d)], self.r2.at[1, d - 1], pc.dev(y=pc.ys(d))))

    def finish(self):
        pc, acc, r2 = self.pc, self.acc, self.r2
        received(self.two)
        own0 = acc[0, pc.x] + r2[0, 0] + r2[0, 1] + r2[0, 2]
        own1 = acc[1, pc.y] + r2[1, 0] + r2[1, 1] + r2[1, 2]
        return own0, own1


def factor_block(load, tick):
    groups = 16
    a = [load(r) for r in range(groups)]
    lane = lax.broadcasted_iota(jnp.int32, (8, 128), 1)
    sub = lax.broadcasted_iota(jnp.int32, (8, 128), 0)
    out = [None] * groups

    def column(v, j):
        return jnp.broadcast_to(v[:, j:j + 1], (8, 128))

    for q in range(32):
        r0, s0, j0 = q // 2, 4 * (q % 2), 4 * q
        rows = [jnp.broadcast_to(a[r0][s0 + s:s0 + s + 1, :], (8, 128)) for s in range(4)]
        p = {(s, t): column(rows[s], j0 + t) for s in range(4) for t in range(s, 4)}
        inside = (lane >= j0) & (lane < j0 + 4)
        v = [jnp.where(inside, jnp.where(lane == j0 + s, 1.0, 0.0), rows[s]) for s in range(4)]
        low, inv = {}, []
        for s in range(4):
            inv.append(1.0 / p[s, s])
            for t in range(s + 1, 4):
                low[t, s] = p[s, t] * inv[s]
            for u in range(s + 1, 4):
                for t in range(u, 4):
                    p[u, t] = p[u, t] - low[u, s] * p[s, t]
        for t in range(1, 4):
            for s in range(t):
                v[t] = v[t] - low[t, s] * v[s]
        w = [v[s] * inv[s] for s in range(4)]
        for s in (2, 1, 0):
            for t in range(s + 1, 4):
                w[s] = w[s] - low[t, s] * w[t]
        done = [v[s] * lax.rsqrt(p[s, s]) for s in range(4)]
        o = done[0]
        for s in range(1, 4):
            o = jnp.where(sub == s0 + s, done[s], o)
        out[r0] = o if s0 == 0 else jnp.where(sub < 4, out[r0], o)
        for r in range(r0 if s0 == 0 else r0 + 1, groups):
            cols = [column(a[r], j0 + t) for t in range(4)]
            new = jnp.where(inside, 0.0, a[r])
            for s in range(4):
                new = new - cols[s] * w[s]
            a[r] = new
        tick(q)
    return out


def kernel(
    grad, mom, rb, update, momentum_next, basis_next,
    blend, blend_send, basis, lpart, lrecv, left, perm,
    gbuf, gr1, gacc, gr2, zbuf, gfull,
    wbuf, wr1, wacc, wr2, wall, left_all,
    work, ybuf, tri, right, orth, sums, squares,
    send_sem, recv_sem,
):
    pc = Place(send_sem, recv_sem)
    c, x, y, z = pc.c, pc.x, pc.y, pc.z
    peers = [pc.partner()]
    peers += [pc.dev(x=pc.xs(d)) for d in (1, 2, 3)]
    peers += [pc.dev(y=pc.ys(d)) for d in (1, 2, 3)]
    peers += [pc.dev(z=pc.zs(d)) for d in range(1, 8)]
    pc.barrier(peers)

    basis_swap = pc.copy(rb.at[1 - c], basis.at[y, x, c], pc.partner())
    basis[y, x, c] = rb[c]
    basis_swap.wait_recv()
    gather = Gather(pc, basis)
    gather.first()
    blend_send[...] = mom[1 - c] + grad[1 - c].astype(F32)
    blend_swap = pc.copy(blend_send, blend.at[c], pc.partner())
    blend[c] = mom[c] + grad[c].astype(F32)
    gather.second()
    at = lax.broadcasted_iota(jnp.int32, (RANK, RANK), 0)
    group, half = at // 128, (at // 64) % 2
    index, low = (at // 16) % 4, at % 16
    py = jnp.where(half == 0, (y + group) % 4, index)
    px = jnp.where(half == 0, index, (x + group) % 4)
    rank = ((py * 4 + px) * 2 + half) * 16 + low
    perm[...] = jnp.where(lax.broadcasted_iota(jnp.int32, (RANK, RANK), 1) == rank, 1.0, 0.0)
    blend_swap.wait_recv()
    sums_in = []
    for d in (0, 3, 1, 2):
        if d:
            received(gather.two[4 - d])
        rows = jnp.concatenate(
            [basis[pc.ys(d), :, 0].reshape(64, 1024), basis[:, pc.xs(d), 1].reshape(64, 1024)], axis=0
        )
        part = dot(blend[...].reshape(512, 1024), rows, 1, 1, HIGH)
        lpart[d] = part.reshape(8, 64, 128)
        for e in (4, 3, 5, 2, 6, 1, 7):
            sums_in.append(pc.copy(lpart.at[d, pc.zs(e)], lrecv.at[e - 1, d], pc.dev(z=pc.zs(e))))
    received(sums_in)
    own = []
    for d in range(4):
        s = lpart[d, z]
        for e in range(7):
            s = s + lrecv[e, d]
        own.append(s)
    own = dot(jnp.concatenate(own, axis=1), perm[...], 1, 0, HIGHEST)
    left[z] = own

    def ring(step):
        up, down = pc.dev(z=pc.zs(1)), pc.dev(z=pc.zs(7))
        a, b = left.at[pc.zs(9 - step)], left.at[pc.zs(step - 1)]
        if step == 4:
            a, b = a.at[pl.ds(0, 32)], b.at[pl.ds(32, 32)]
        return [pc.copy(a, a, up), pc.copy(b, b, down)]

    blocks = []
    for i in range(4):
        row = dot(own[:, 128 * i:128 * i + 128], own[:, :128 * i + 128], 0, 0, HIGHEST)
        blocks += [row[:, 128 * j:128 * j + 128] for j in range(i + 1)]
    gbuf[...] = jnp.concatenate(blocks, axis=0).reshape(4, 4, 2, 40, 128)
    gscatter = Scatter(pc, gbuf, gr1, gacc, gr2)
    gscatter.first()
    lefts = ring(1)
    gscatter.second()
    received(lefts)
    lefts = ring(2)
    own0, own1 = gscatter.finish()
    zbuf[z, 0] = own0
    zbuf[z, 1] = own1
    zs = []
    for d in (4, 3, 5, 2, 6, 1, 7):
        zs.append(pc.copy(zbuf.at[z], zbuf.at[z], pc.dev(z=pc.zs(d))))
    received(lefts)
    lefts = ring(3)
    received(zs)
    total = zbuf[0]
    for d in range(1, 8):
        total = total + zbuf[d]
    gfull[y, x] = total
    ggather = Gather(pc, gfull)
    ggather.first()
    received(lefts)
    lefts = ring(4)
    ggather.second()
    received(lefts)
    for i in range(4):
        lt = left[:, :, 128 * i:128 * i + 128].reshape(RANK, 128)
        part = dot(lt, blend[...].reshape(512, 1024), 0, 0, HIGH)
        wbuf[i] = part.reshape(4, 2, 16, 1024)
    wscatter = Scatter(pc, wbuf, wr1, wacc, wr2)
    wscatter.first()
    left_all[c] = left[pl.ds(4 * c, 4)]
    left_swap = pc.copy(left.at[pl.ds(4 * (1 - c), 4)], left_all.at[c], pc.partner())
    ggather.finish()

    wgather = Gather(pc, wall.at[c])
    w_swaps = []

    def w_second():
        wscatter.second()

    def w_gather():
        o0, o1 = wscatter.finish()
        wall[c, y, x, 0] = o0
        wall[c, y, x, 1] = o1
        wgather.first()

    def w_gather_second():
        wgather.second()
        for a in (wall.at[c, y, :, 0], wall.at[c, :, x, 1]):
            w_swaps.append(pc.copy(a, a, pc.partner()))

    def w_last():
        for d in (1, 3, 2):
            received(wgather.two[d])
            for a in (wall.at[c, pc.ys(4 - d), :, 0], wall.at[c, :, pc.xs(4 - d), 1]):
                w_swaps.append(pc.copy(a, a, pc.partner()))

    events = {(1, 16): w_second, (2, 2): w_gather, (2, 20): w_gather_second}
    flat = gfull[...].reshape(1280, 128)
    for b in range(10):
        work[b] = flat[128 * b:128 * b + 128]
    at = lambda i, j: i * (i + 1) // 2 + j
    yat = lambda i, j: i * (i - 1) // 2 + j
    rowi = lax.broadcasted_iota(jnp.int32, (128, 128), 0)
    coli = lax.broadcasted_iota(jnp.int32, (128, 128), 1)
    tri_swaps = []
    pending = []

    def tri_row(k, inv):
        for j in range(4):
            cols = pl.ds(128 * j, 128)
            if j < k:
                tri[c, pl.ds(128 * k, 128), cols] = dot(inv, ybuf[yat(k, j)], 1, 0, HIGHEST)
            elif j == k:
                tri[c, pl.ds(128 * k, 128), cols] = inv
            else:
                tri[c, pl.ds(128 * k, 128), cols] = jnp.zeros((128, 128), F32)
        a = tri.at[c, pl.ds(128 * k, 128)]
        tri_swaps.append(pc.copy(a, a, pc.partner()))

    def later(k, inv):
        def solve(i):
            work[at(i, k)] = dot(work[at(i, k)], inv, 1, 1, HIGHEST)

        def trail(i, j):
            work[at(i, j)] = work[at(i, j)] - dot(work[at(i, k)], work[at(j, k)], 1, 1, HIGHEST)

        def inverse(i, j):
            new = dot(work[at(i, k)], tri[c, pl.ds(128 * k, 128), pl.ds(128 * j, 128)], 1, 0, HIGHEST)
            ybuf[yat(i, j)] = -new if j == k else ybuf[yat(i, j)] - new

        jobs = [lambda: tri_row(k, inv)]
        for i in range(k + 2, 4):
            jobs.append(lambda i=i: solve(i))
        for i in range(k + 2, 4):
            for j in range(k + 1, i + 1):
                jobs.append(lambda i=i, j=j: trail(i, j))
        for i in range(k + 1, 4):
            for j in range(k + 1):
                jobs.append(lambda i=i, j=j: inverse(i, j))
        return jobs

    for k in range(4):

        def tick(q, k=k):
            if (k, q) in events:
                events[k, q]()
            if pending and q >= 1:
                pending.pop(0)()

        rows = factor_block(lambda r: work[at(k, k), 8 * r:8 * r + 8, :], tick)
        while pending:
            pending.pop(0)()
        inv = jnp.where(rowi >= coli, jnp.concatenate(rows, axis=0), 0.0)
        if k < 3:
            below = dot(work[at(k + 1, k)], inv, 1, 1, HIGHEST)
            work[at(k + 1, k)] = below
            work[at(k + 1, k + 1)] = work[at(k + 1, k + 1)] - dot(below, below, 1, 1, HIGHEST)
            pending = later(k, inv)
        else:
            tri_row(k, inv)
    w_last()

    def raw(m):
        def part(j, carry):
            cols = pl.ds(pl.multiple_of(j * 256, 256), 256)
            wj = wall[m, :, :, :, :, cols].reshape(RANK, 256)
            for i in range(4):
                n = 128 * (i + 1)
                t = tri[m, pl.ds(128 * i, 128), pl.ds(0, n)]
                right[m, pl.ds(128 * i, 128), cols] = dot(t, wj[:n], 1, 0, HIGH)
            return carry

        lax.fori_loop(0, 4, part, 0)
        r = right[m]
        sums[m] = dot(jnp.ones((8, 1024), F32), r * r, 1, 1, HIGHEST)

    raw(c)
    received(w_swaps)
    received(tri_swaps)
    raw(1 - c)
    left_swap.wait_recv()
    pieces = [sums[m, 0:1, 128 * j:128 * j + 128] for m in range(2) for j in range(4)]
    squares[z] = jnp.concatenate(pieces, axis=0)
    zs = []
    for d in (4, 3, 5, 2, 6, 1, 7):
        zs.append(pc.copy(squares.at[z], squares.at[z], pc.dev(z=pc.zs(d))))
    for m in range(2):
        orth[m] = dot(left_all[m].reshape(256, RANK), tri[m], 1, 1, HIGH)

        def feed(j, carry, m=m):
            cols = pl.ds(pl.multiple_of(j * 256, 256), 256)
            back = dot(orth[m], right[m, :, cols], 1, 0, HIGH)
            blended = mom[m, :, cols] + grad[m, :, cols].astype(F32)
            momentum_next[m, :, cols] = blended - (1.0 - momentum_decay) * back
            return carry

        lax.fori_loop(0, 4, feed, 0)
    received(zs)
    total = squares[0]
    for d in range(1, 8):
        total = total + squares[d]
    inverse = lax.rsqrt(total / D + epsilon_sq)
    lane = lax.broadcasted_iota(jnp.int32, (16, RANK), 1)
    sub = lax.broadcasted_iota(jnp.int32, (16, RANK), 0)
    for m in range(2):
        inv = jnp.concatenate([inverse[4 * m + j:4 * m + j + 1] for j in range(4)], axis=1)
        orth[m] = orth[m] * inv
        pick = jnp.where(lane == pc.f * 16 + sub, inv, 0.0)

        def direction(j, carry, m=m, pick=pick):
            cols = pl.ds(pl.multiple_of(j * 256, 256), 256)
            rj = right[m, :, cols]
            out = math.sqrt(D / RANK) * dot(orth[m], rj, 1, 0, HIGH)
            update[m, :, cols] = out.astype(jnp.bfloat16)
            basis_next[m, :, cols] = dot(pick, rj, 1, 0, HIGHEST)
            return carry

        lax.fori_loop(0, 4, direction, 0)
    pc.drain()


def shards(gradient, momentum, right_basis):
    vmem = pl.BlockSpec(memory_space=pltpu.VMEM)
    shape = lambda s: jax.ShapeDtypeStruct(s, F32)
    buf = lambda *s: pltpu.VMEM(s, F32)
    n = 126
    return pl.pallas_call(
        kernel,
        out_shape=(
            jax.ShapeDtypeStruct((2, 256, 1024), jnp.bfloat16), shape((2, 256, 1024)), shape((2, 16, 1024))
        ),
        in_specs=[vmem] * 3,
        out_specs=[vmem] * 3,
        scratch_shapes=[
            buf(2, 256, 1024), buf(256, 1024), buf(4, 4, 2, 16, 1024),
            buf(4, 8, 64, 128), buf(7, 4, 64, 128), buf(8, 64, RANK), buf(RANK, RANK),
            buf(4, 4, 2, 40, 128), buf(2, 3, 4, 40, 128), buf(2, 4, 40, 128), buf(2, 3, 40, 128),
            buf(8, 2, 40, 128), buf(4, 4, 2, 40, 128),
            buf(4, 4, 2, 16, 1024), buf(2, 3, 4, 16, 1024), buf(2, 4, 16, 1024), buf(2, 3, 16, 1024),
            buf(2, 4, 4, 2, 16, 1024), buf(2, 4, 64, RANK),
            buf(10, 128, 128), buf(6, 128, 128), buf(2, RANK, RANK),
            buf(2, RANK, 1024), buf(2, 256, RANK), buf(2, 8, RANK), buf(8, 8, 128),
            pltpu.SemaphoreType.DMA((n,)), pltpu.SemaphoreType.DMA((n,)),
        ],
        compiler_params=pltpu.CompilerParams(
            collective_id=0, has_side_effects=True, vmem_limit_bytes=VMEM_BYTES
        ),
        name="dion",
    )(gradient, momentum, right_basis)


def solution(mesh):
    placed = (P(None, "fsdp", "tp"), P(None, "fsdp", "tp"), P(None, "fsdp", "tp"))
    return jax.shard_map(
        shards,
        mesh=mesh,
        in_specs=placed,
        out_specs=placed,
        check_vma=False,
    )
```

time: 219 us -> 142 us (0.65)
  Pallas kernels: 214 us -> 137 us
    pallas_call x3 -> x1, Pallas kernels: 214 us -> 137 us  [shards(): pl.pallas_call(kernel, out_shape=(jax.ShapeDtypeStruct((2, 256, 1024), jn...]
where the time goes in v2:
time: 142 us
  Pallas kernels  137 us (96%)
  local copies, waits for them, and re-layouts  4.39 us (3%)
    pallas_call x1, Pallas kernels, shards(): pl.pallas_call(kernel, out_shape=(jax.ShapeDtypeStruct((2, 256, 1024), jn...  137 us
    unnamed x7, local copies, waits for them, and re-layouts  4.39 us

profile of v2, /device:TPU:1, one launch (start us, length us, event | category | flops | bytes accessed | tf_op | source)
XLA Modules:
  0.0 141.7 jit_solution(2537215868406084532)
XLA Ops:
  0.6 136.7 %dion.1 = (bf16[2,256,1024]{2,1,0:T(8,128)(2,1)}, f32[2,256,1024]{2,1,0:T(8,128)}, f32[2,16,1024]{2,1,0:T(8,128)}) custom-call(bf16[2,256,1024]{2,1,0:T(8,128)(2,1)} %grad.1, f32[2,256,1024]{2,1,0:T(8,128)} %mom.1, f32[2,16,1024]{2,1,0:T(8,128)} %rb.1), custom_call_target="tpu_custom_call" | custom-call | tf_op jit(solution)/shard_map/dion/pallas_call | solution.py:444
  137.3 0.0 copy-start
  137.3 2.4 %copy.9 = bf16[2,256,1024]{2,1,0:T(8,128)(2,1)} copy(bf16[2,256,1024]{2,1,0:T(8,128)(2,1)} %get-tuple-element.6) | data formatting | bytes 2097152
  139.7 0.0 copy-done
  139.7 0.0 copy-start.1
  139.7 1.3 copy.10
  141.0 0.0 copy-done.1
  141.0 0.7 copy.11
Async XLA Ops:
  137.3 2.4 %copy-start = (f32[2,256,1024]{2,1,0:T(8,128)S(1)}, f32[2,256,1024]{2,1,0:T(8,128)}, u32[]{:S(2)}) copy-start(f32[2,256,1024]{2,1,0:T(8,128)} %get-tuple-element.7) | copy-start | bytes 6291460
  139.7 1.3 copy-start.1

commit v3 on v2

--- a/solution.py
+++ b/solution.py
@@ -151,38 +151,61 @@
     def column(v, j):
         return jnp.broadcast_to(v[:, j:j + 1], (8, 128))
 
+    def recip(v):
+        return pl.reciprocal(v, approx=True)
+
     for q in range(32):
         r0, s0, j0 = q // 2, 4 * (q % 2), 4 * q
         rows = [jnp.broadcast_to(a[r0][s0 + s:s0 + s + 1, :], (8, 128)) for s in range(4)]
         p = {(s, t): column(rows[s], j0 + t) for s in range(4) for t in range(s, 4)}
         inside = (lane >= j0) & (lane < j0 + 4)
-        v = [jnp.where(inside, jnp.where(lane == j0 + s, 1.0, 0.0), rows[s]) for s in range(4)]
-        low, inv = {}, []
+        sc = [lax.rsqrt(p[s, s]) for s in range(4)]
+        v = [jnp.where(inside, jnp.where(lane == j0 + s, 1.0, 0.0), rows[s]) * sc[s] for s in range(4)]
+        r = {(s, t): p[s, t] * (sc[s] * sc[t]) for s in range(4) for t in range(s + 1, 4)}
+        l10, l20, l30 = r[0, 1], r[0, 2], r[0, 3]
+        u11, u22, u33 = 1.0 - l10 * l10, 1.0 - l20 * l20, 1.0 - l30 * l30
+        u12, u13, u23 = r[1, 2] - l10 * l20, r[1, 3] - l10 * l30, r[2, 3] - l20 * l30
+        v22, v23, v33 = u11 * u22 - u12 * u12, u11 * u23 - u12 * u13, u11 * u33 - u13 * u13
+        w33 = v22 * v33 - v23 * v23
+        i1, i2, i3 = recip(u11), recip(v22), recip(w33)
+        l21, l31, l32 = u12 * i1, u13 * i1, v23 * i2
+        d1, d2, d3 = i1, u11 * i2, (u11 * v22) * i3
+        n10, n21, n32 = -l10, -l21, -l32
+        n20 = l21 * l10 - l20
+        n31 = l32 * l21 - l31
+        n30 = l31 * l10 - l30 - l32 * n20
+        n = [[None] * 4, [n10], [n20, n21], [n30, n31, n32]]
+        m = {}
+        e1 = d1 * n10
+        e20, e21 = d2 * n20, d2 * n21
+        m[0, 0] = (1.0 + e1 * n10 + e20 * n20) + d3 * (n30 * n30)
+        m[0, 1] = (e1 + e20 * n21) + d3 * (n30 * n31)
+        m[0, 2] = e20 + d3 * (n30 * n32)
+        m[0, 3] = d3 * n30
+        m[1, 1] = (d1 + e21 * n21) + d3 * (n31 * n31)
+        m[1, 2] = e21 + d3 * (n31 * n32)
+        m[1, 3] = d3 * n31
+        m[2, 2] = d2 + d3 * (n32 * n32)
+        m[2, 3] = d3 * n32
+        m[3, 3] = d3
+        w = []
         for s in range(4):
-            inv.append(1.0 / p[s, s])
-            for t in range(s + 1, 4):
-                low[t, s] = p[s, t] * inv[s]
-            for u in range(s + 1, 4):
-                for t in range(u, 4):
-                    p[u, t] = p[u, t] - low[u, s] * p[s, t]
-        for t in range(1, 4):
-            for s in range(t):
-                v[t] = v[t] - low[t, s] * v[s]
-        w = [v[s] * inv[s] for s in range(4)]
-        for s in (2, 1, 0):
-            for t in range(s + 1, 4):
-                w[s] = w[s] - low[t, s] * w[t]
-        done = [v[s] * lax.rsqrt(p[s, s]) for s in range(4)]
+            t = [m[min(s, t), max(s, t)] * v[t] for t in range(4)]
+            w.append(((t[0] + t[1]) + (t[2] + t[3])) * sc[s])
+        f = [None, d1 * lax.rsqrt(d1), d2 * lax.rsqrt(d2), d3 * lax.rsqrt(d3)]
+        done = [v[0]]
+        for s in range(1, 4):
+            t = v[s]
+            for k in range(s):
+                t = t + n[s][k] * v[k]
+            done.append(f[s] * t)
         o = done[0]
         for s in range(1, 4):
             o = jnp.where(sub == s0 + s, done[s], o)
         out[r0] = o if s0 == 0 else jnp.where(sub < 4, out[r0], o)
-        for r in range(r0 if s0 == 0 else r0 + 1, groups):
-            cols = [column(a[r], j0 + t) for t in range(4)]
-            new = jnp.where(inside, 0.0, a[r])
-            for s in range(4):
-                new = new - cols[s] * w[s]
-            a[r] = new
+        for g in range(r0 if s0 == 0 else r0 + 1, groups):
+            t = [column(a[g], j0 + t) * w[t] for t in range(4)]
+            a[g] = jnp.where(inside, 0.0, a[g]) - ((t[0] + t[1]) + (t[2] + t[3]))
         tick(q)
     return out
 
@@ -311,7 +334,7 @@
             for a in (wall.at[c, pc.ys(4 - d), :, 0], wall.at[c, :, pc.xs(4 - d), 1]):
                 w_swaps.append(pc.copy(a, a, pc.partner()))
 
-    events = {(1, 16): w_second, (2, 2): w_gather, (2, 20): w_gather_second}
+    events = {(1, 24): w_second, (2, 12): w_gather, (2, 30): w_gather_second}
     flat = gfull[...].reshape(1280, 128)
     for b in range(10):
         work[b] = flat[128 * b:128 * b + 128]
@@ -388,8 +411,10 @@
             return carry
 
         lax.fori_loop(0, 4, part, 0)
-        r = right[m]
-        sums[m] = dot(jnp.ones((8, 1024), F32), r * r, 1, 1, HIGHEST)
+        fold = right[m, :, 0:128] * right[m, :, 0:128]
+        for j in range(1, 8):
+            fold = fold + right[m, :, 128 * j:128 * j + 128] * right[m, :, 128 * j:128 * j + 128]
+        sums[m] = dot(jnp.ones((8, 128), F32), fold, 1, 1, HIGHEST)
 
     raw(c)
     received(w_swaps)
@@ -422,18 +447,32 @@
     for m in range(2):
         inv = jnp.concatenate([inverse[4 * m + j:4 * m + j + 1] for j in range(4)], axis=1)
         orth[m] = orth[m] * inv
-        pick = jnp.where(lane == pc.f * 16 + sub, inv, 0.0)
-
-        def direction(j, carry, m=m, pick=pick):
+        pick = jnp.sum(jnp.where(lane == pc.f * 16 + sub, inv, 0.0), axis=1, keepdims=True)
+        basis_next[m] = right[m, pl.ds(pl.multiple_of(pc.f * 16, 16), 16), :] * pick
+
+        def direction(j, carry, m=m):
             cols = pl.ds(pl.multiple_of(j * 256, 256), 256)
             rj = right[m, :, cols]
             out = math.sqrt(D / RANK) * dot(orth[m], rj, 1, 0, HIGH)
             update[m, :, cols] = out.astype(jnp.bfloat16)
-            basis_next[m, :, cols] = dot(pick, rj, 1, 0, HIGHEST)
             return carry
 
         lax.fori_loop(0, 4, direction, 0)
     pc.drain()
+
+
+def place_kernel(update, momentum_next, basis_next, update_out, momentum_out, basis_out, sem):
+    pairs = [(basis_next.at[m], basis_out.at[m]) for m in range(2)]
+    for m in range(2):
+        for i in range(2):
+            rows = pl.ds(128 * i, 128)
+            pairs.append((momentum_next.at[m, rows], momentum_out.at[m, rows]))
+            pairs.append((update.at[m, rows], update_out.at[m, rows]))
+    copies = [pltpu.make_async_copy(a, b, sem.at[i]) for i, (a, b) in enumerate(pairs)]
+    for cp in copies:
+        cp.start()
+    for cp in copies:
+        cp.wait()
 
 
 def shards(gradient, momentum, right_basis):
@@ -441,7 +480,7 @@
     shape = lambda s: jax.ShapeDtypeStruct(s, F32)
     buf = lambda *s: pltpu.VMEM(s, F32)
     n = 126
-    return pl.pallas_call(
+    results = pl.pallas_call(
         kernel,
         out_shape=(
             jax.ShapeDtypeStruct((2, 256, 1024), jnp.bfloat16), shape((2, 256, 1024)), shape((2, 16, 1024))
@@ -464,6 +503,16 @@
         ),
         name="dion",
     )(gradient, momentum, right_basis)
+    anywhere = pl.BlockSpec(memory_space=pl.ANY)
+    return pl.pallas_call(
+        place_kernel,
+        out_shape=tuple(jax.ShapeDtypeStruct(r.shape, r.dtype) for r in results),
+        in_specs=[anywhere] * 3,
+        out_specs=[anywhere] * 3,
+        scratch_shapes=[pltpu.SemaphoreType.DMA((10,))],
+        compiler_params=pltpu.CompilerParams(has_side_effects=True),
+        name="place",
+    )(*results)
 
 
 def solution(mesh):

time: 142 us -> 236 us (1.66)
  Pallas kernels: 137 us -> 236 us
  local copies, waits for them, and re-layouts: 4.39 us -> 0 us
    pallas_call x0 -> x1, Pallas kernels: none -> 100 us  [shards(): pl.pallas_call(place_kernel, out_shape=tuple((jax.ShapeDtypeStruct(r.shap...]
    unnamed x7 -> x0, local copies, waits for them, and re-layouts: 4.39 us -> none
where the time goes in v3:
time: 236 us
  Pallas kernels  236 us (100%)
    pallas_call x1, Pallas kernels, shards(): pl.pallas_call(kernel, out_shape=(jax.ShapeDtypeStruct((2, 256, 1024), jn...  135 us
    pallas_call x1, Pallas kernels, shards(): pl.pallas_call(place_kernel, out_shape=tuple((jax.ShapeDtypeStruct(r.shap...  100 us

profile of v3, /device:TPU:1, one launch (start us, length us, event | category | flops | bytes accessed | tf_op | source)
XLA Modules:
  0.0 236.4 jit_solution(16956860287503539329)
XLA Ops:
  0.6 135.1 %dion.1 = (bf16[2,256,1024]{2,1,0:T(8,128)(2,1)}, f32[2,256,1024]{2,1,0:T(8,128)}, f32[2,16,1024]{2,1,0:T(8,128)}) custom-call(bf16[2,256,1024]{2,1,0:T(8,128)(2,1)} %grad.1, f32[2,256,1024]{2,1,0:T(8,128)} %mom.1, f32[2,16,1024]{2,1,0:T(8,128)} %rb.1), custom_call_target="tpu_custom_call" | custom-call | tf_op jit(solution)/shard_map/dion/pallas_call | solution.py:483
  135.8 100.5 %place.1 = (bf16[2,256,1024]{2,1,0:T(8,128)(2,1)}, f32[2,256,1024]{2,1,0:T(8,128)}, f32[2,16,1024]{2,1,0:T(8,128)}) custom-call(bf16[2,256,1024]{2,1,0:T(8,128)(2,1)} %get-tuple-element.6.update, f32[2,256,1024]{2,1,0:T(8,128)} %get-tuple-element.7.momentum_next, f32[2,16,1024]{2,1,0:T(8,128)} %get-tuple-element.8.basis_next), custom_call_target="tpu_custom_call" | custom-call | tf_op jit(solution)/shard_map/place/pallas_call | solution.py:507

commit v4 on v3

--- a/solution.py
+++ b/solution.py
@@ -55,14 +55,19 @@
     def zs(self, d):
         return lax.rem(self.z + d, 8)
 
-    def copy(self, src, dst, to):
+    def reserve(self, n):
         i = self.count
-        self.count += 1
+        self.count += n
+        assert self.count <= self.send_sem.shape[0]
+        return i
+
+    def copy(self, src, dst, to, recv=None):
+        i = self.reserve(1)
         cp = pltpu.make_async_remote_copy(
             src_ref=src,
             dst_ref=dst,
             send_sem=self.send_sem.at[i],
-            recv_sem=self.recv_sem.at[i],
+            recv_sem=self.recv_sem.at[i if recv is None else recv],
             device_id=to,
             device_id_type=MESH,
         )
@@ -212,28 +217,58 @@
 
 def kernel(
     grad, mom, rb, update, momentum_next, basis_next,
-    blend, blend_send, basis, lpart, lrecv, left, perm,
-    gbuf, gr1, gacc, gr2, zbuf, gfull,
+    gv, mv, upd, bnext, blend, blend_send, basis, lpart, lrecv, left, perm,
+    gbuf, gr1, gacc, gr2, zsrc, zpart, zfull, gfull,
     wbuf, wr1, wacc, wr2, wall, left_all,
     work, ybuf, tri, right, orth, sums, squares,
-    send_sem, recv_sem,
+    send_sem, recv_sem, local_sem,
 ):
     pc = Place(send_sem, recv_sem)
     c, x, y, z = pc.c, pc.x, pc.y, pc.z
+    loads = []
+    for i, m in enumerate((1 - c, c)):
+        loads.append(
+            (
+                pltpu.make_async_copy(mom.at[m], mv.at[m], local_sem.at[2 * i]),
+                pltpu.make_async_copy(grad.at[m], gv.at[m], local_sem.at[2 * i + 1]),
+            )
+        )
+        for cp in loads[i]:
+            cp.start()
     peers = [pc.partner()]
-    peers += [pc.dev(x=pc.xs(d)) for d in (1, 2, 3)]
-    peers += [pc.dev(y=pc.ys(d)) for d in (1, 2, 3)]
+    peers += [pc.dev(x=pc.xs(d), c=m) for d in (1, 2, 3) for m in (0, 1)]
+    peers += [pc.dev(y=pc.ys(d), c=m) for d in (1, 2, 3) for m in (0, 1)]
     peers += [pc.dev(z=pc.zs(d)) for d in range(1, 8)]
     pc.barrier(peers)
 
+    first = pc.reserve(6)
+    slot = lambda d, h: first + 2 * (d - 1) + h
+    for d in (1, 3, 2):
+        to_y, to_x = lax.rem(y + d * c, 4), lax.rem(x + d * (1 - c), 4)
+        for m in range(2):
+            pc.copy(rb.at[m], basis.at[y, x, c], pc.dev(y=to_y, x=to_x, c=m), recv=slot(d, c))
     basis_swap = pc.copy(rb.at[1 - c], basis.at[y, x, c], pc.partner())
     basis[y, x, c] = rb[c]
+    for cp in loads[0]:
+        cp.wait()
+    blend_send[...] = mv[1 - c] + gv[1 - c].astype(F32)
+    blend_swap = pc.copy(blend_send, blend.at[c], pc.partner())
+    for cp in loads[1]:
+        cp.wait()
+    blend[c] = mv[c] + gv[c].astype(F32)
     basis_swap.wait_recv()
+    for d in (1, 3, 2):
+        for h in range(2):
+            pltpu.make_async_remote_copy(
+                src_ref=rb.at[0],
+                dst_ref=basis.at[y, x, h],
+                send_sem=send_sem.at[slot(d, h)],
+                recv_sem=recv_sem.at[slot(d, h)],
+                device_id=pc.partner(),
+                device_id_type=MESH,
+            ).wait_recv()
     gather = Gather(pc, basis)
-    gather.first()
-    blend_send[...] = mom[1 - c] + grad[1 - c].astype(F32)
-    blend_swap = pc.copy(blend_send, blend.at[c], pc.partner())
-    blend[c] = mom[c] + grad[c].astype(F32)
+    gather.one = []
     gather.second()
     at = lax.broadcasted_iota(jnp.int32, (RANK, RANK), 0)
     group, half = at // 128, (at // 64) % 2
@@ -262,14 +297,18 @@
             s = s + lrecv[e, d]
         own.append(s)
     own = dot(jnp.concatenate(own, axis=1), perm[...], 1, 0, HIGHEST)
-    left[z] = own
+    for q in range(2):
+        left[q, z] = own[:, 256 * q:256 * q + 256]
 
     def ring(step):
         up, down = pc.dev(z=pc.zs(1)), pc.dev(z=pc.zs(7))
-        a, b = left.at[pc.zs(9 - step)], left.at[pc.zs(step - 1)]
-        if step == 4:
-            a, b = a.at[pl.ds(0, 32)], b.at[pl.ds(32, 32)]
-        return [pc.copy(a, a, up), pc.copy(b, b, down)]
+        copies = []
+        for q in range(2):
+            a, b = left.at[q, pc.zs(9 - step)], left.at[q, pc.zs(step - 1)]
+            if step == 4:
+                a, b = a.at[pl.ds(0, 32)], b.at[pl.ds(32, 32)]
+            copies += [pc.copy(a, a, up), pc.copy(b, b, down)]
+        return copies
 
     blocks = []
     for i in range(4):
@@ -283,58 +322,76 @@
     received(lefts)
     lefts = ring(2)
     own0, own1 = gscatter.finish()
-    zbuf[z, 0] = own0
-    zbuf[z, 1] = own1
+    zsrc[0:5] = jnp.concatenate([own0, own1], axis=0).reshape(5, 16, 128)
+    zsrc[5:8] = jnp.zeros((3, 16, 128), F32)
     zs = []
     for d in (4, 3, 5, 2, 6, 1, 7):
-        zs.append(pc.copy(zbuf.at[z], zbuf.at[z], pc.dev(z=pc.zs(d))))
+        zs.append(pc.copy(zsrc.at[pc.zs(d)], zpart.at[d - 1], pc.dev(z=pc.zs(d))))
     received(lefts)
     lefts = ring(3)
     received(zs)
-    total = zbuf[0]
-    for d in range(1, 8):
-        total = total + zbuf[d]
-    gfull[y, x] = total
+    total = zsrc[z]
+    for d in range(7):
+        total = total + zpart[d]
+    zfull[z] = total
+    zs = []
+    for d in (4, 3, 5, 2, 6, 1, 7):
+        zs.append(pc.copy(zfull.at[z], zfull.at[z], pc.dev(z=pc.zs(d))))
+    received(lefts)
+    lefts = ring(4)
+    received(zs)
+    gfull[y, x] = zfull[0:5].reshape(2, 40, 128)
     ggather = Gather(pc, gfull)
     ggather.first()
     received(lefts)
-    lefts = ring(4)
     ggather.second()
-    received(lefts)
-    for i in range(4):
-        lt = left[:, :, 128 * i:128 * i + 128].reshape(RANK, 128)
-        part = dot(lt, blend[...].reshape(512, 1024), 0, 0, HIGH)
-        wbuf[i] = part.reshape(4, 2, 16, 1024)
-    wscatter = Scatter(pc, wbuf, wr1, wacc, wr2)
-    wscatter.first()
-    left_all[c] = left[pl.ds(4 * c, 4)]
-    left_swap = pc.copy(left.at[pl.ds(4 * (1 - c), 4)], left_all.at[c], pc.partner())
+    wscatter, wgather = [], []
+    for q in range(2):
+        for i in range(2):
+            lt = left[q, :, :, 128 * i:128 * i + 128].reshape(RANK, 128)
+            part = dot(lt, blend[...].reshape(512, 1024), 0, 0, HIGH)
+            wbuf[q, 2 * i:2 * i + 2] = part.reshape(2, 4, 2, 8, 1024)
+        wscatter.append(Scatter(pc, wbuf.at[q], wr1.at[q], wacc.at[q], wr2.at[q]))
+        wscatter[q].first()
+        wgather.append(Gather(pc, wall.at[c, q]))
+    left_all[c] = left[:, pl.ds(4 * c, 4)]
+    left_swap = pc.copy(left.at[:, pl.ds(4 * (1 - c), 4)], left_all.at[c], pc.partner())
     ggather.finish()
 
-    wgather = Gather(pc, wall.at[c])
-    w_swaps = []
-
-    def w_second():
-        wscatter.second()
-
-    def w_gather():
-        o0, o1 = wscatter.finish()
-        wall[c, y, x, 0] = o0
-        wall[c, y, x, 1] = o1
-        wgather.first()
-
-    def w_gather_second():
-        wgather.second()
-        for a in (wall.at[c, y, :, 0], wall.at[c, :, x, 1]):
-            w_swaps.append(pc.copy(a, a, pc.partner()))
-
-    def w_last():
+    w_swaps = ([], [])
+
+    def w_gather(q):
+        o0, o1 = wscatter[q].finish()
+        wall[c, q, y, x, 0] = o0
+        wall[c, q, y, x, 1] = o1
+        wgather[q].first()
+
+    def w_gather_second(q):
+        wgather[q].second()
+        for a in (wall.at[c, q, y, :, 0], wall.at[c, q, :, x, 1]):
+            w_swaps[q].append(pc.copy(a, a, pc.partner()))
+
+    def w_last(q):
         for d in (1, 3, 2):
-            received(wgather.two[d])
-            for a in (wall.at[c, pc.ys(4 - d), :, 0], wall.at[c, :, pc.xs(4 - d), 1]):
-                w_swaps.append(pc.copy(a, a, pc.partner()))
-
-    events = {(1, 24): w_second, (2, 12): w_gather, (2, 30): w_gather_second}
+            received(wgather[q].two[d])
+            for a in (wall.at[c, q, pc.ys(4 - d), :, 0], wall.at[c, q, :, pc.xs(4 - d), 1]):
+                w_swaps[q].append(pc.copy(a, a, pc.partner()))
+
+    def w_step1():
+        wscatter[0].second()
+
+    def w_step2():
+        wscatter[1].second()
+        w_gather(0)
+
+    def w_step3():
+        w_gather(1)
+        w_gather_second(0)
+
+    def w_step4():
+        w_gather_second(1)
+
+    events = {(1, 2): w_step1, (1, 28): w_step2, (2, 10): w_step3, (2, 26): w_step4}
     flat = gfull[...].reshape(1280, 128)
     for b in range(10):
         work[b] = flat[128 * b:128 * b + 128]
@@ -398,45 +455,64 @@
             pending = later(k, inv)
         else:
             tri_row(k, inv)
-    w_last()
-
-    def raw(m):
+
+    def raw(m, q):
         def part(j, carry):
             cols = pl.ds(pl.multiple_of(j * 256, 256), 256)
-            wj = wall[m, :, :, :, :, cols].reshape(RANK, 256)
-            for i in range(4):
-                n = 128 * (i + 1)
-                t = tri[m, pl.ds(128 * i, 128), pl.ds(0, n)]
-                right[m, pl.ds(128 * i, 128), cols] = dot(t, wj[:n], 1, 0, HIGH)
+            wj = wall[m, q, :, :, :, :, cols].reshape(256, 256)
+            t = tri[m, pl.ds(256 * q, 512 - 256 * q), pl.ds(256 * q, 256)]
+            new = dot(t, wj, 1, 0, HIGH)
+            if q == 0:
+                right[m, :, cols] = new
+            else:
+                right[m, 256:, cols] = right[m, 256:, cols] + new
             return carry
 
         lax.fori_loop(0, 4, part, 0)
+
+    def squares_of(m):
         fold = right[m, :, 0:128] * right[m, :, 0:128]
         for j in range(1, 8):
             fold = fold + right[m, :, 128 * j:128 * j + 128] * right[m, :, 128 * j:128 * j + 128]
         sums[m] = dot(jnp.ones((8, 128), F32), fold, 1, 1, HIGHEST)
 
-    raw(c)
-    received(w_swaps)
+    w_last(0)
+    raw(c, 0)
+    w_last(1)
+    raw(c, 1)
+    squares_of(c)
     received(tri_swaps)
-    raw(1 - c)
+    received(w_swaps[0])
+    raw(1 - c, 0)
+    received(w_swaps[1])
+    raw(1 - c, 1)
+    squares_of(1 - c)
     left_swap.wait_recv()
     pieces = [sums[m, 0:1, 128 * j:128 * j + 128] for m in range(2) for j in range(4)]
     squares[z] = jnp.concatenate(pieces, axis=0)
     zs = []
     for d in (4, 3, 5, 2, 6, 1, 7):
         zs.append(pc.copy(squares.at[z], squares.at[z], pc.dev(z=pc.zs(d))))
+    stores = []
+
+    def store(src, dst):
+        cp = pltpu.make_async_copy(src, dst, local_sem.at[4 + len(stores)])
+        cp.start()
+        stores.append(cp)
+
     for m in range(2):
-        orth[m] = dot(left_all[m].reshape(256, RANK), tri[m], 1, 1, HIGH)
+        rows = jnp.concatenate([left_all[m, q].reshape(256, 256) for q in range(2)], axis=1)
+        orth[m] = dot(rows, tri[m], 1, 1, HIGH)
 
         def feed(j, carry, m=m):
             cols = pl.ds(pl.multiple_of(j * 256, 256), 256)
             back = dot(orth[m], right[m, :, cols], 1, 0, HIGH)
-            blended = mom[m, :, cols] + grad[m, :, cols].astype(F32)
-            momentum_next[m, :, cols] = blended - (1.0 - momentum_decay) * back
+            blended = mv[m, :, cols] + gv[m, :, cols].astype(F32)
+            mv[m, :, cols] = blended - (1.0 - momentum_decay) * back
             return carry
 
         lax.fori_loop(0, 4, feed, 0)
+        store(mv.at[m], momentum_next.at[m])
     received(zs)
     total = squares[0]
     for d in range(1, 8):
@@ -448,69 +524,79 @@
         inv = jnp.concatenate([inverse[4 * m + j:4 * m + j + 1] for j in range(4)], axis=1)
         orth[m] = orth[m] * inv
         pick = jnp.sum(jnp.where(lane == pc.f * 16 + sub, inv, 0.0), axis=1, keepdims=True)
-        basis_next[m] = right[m, pl.ds(pl.multiple_of(pc.f * 16, 16), 16), :] * pick
+        bnext[m] = right[m, pl.ds(pl.multiple_of(pc.f * 16, 16), 16), :] * pick
+        store(bnext.at[m], basis_next.at[m])
 
         def direction(j, carry, m=m):
             cols = pl.ds(pl.multiple_of(j * 256, 256), 256)
-            rj = right[m, :, cols]
-            out = math.sqrt(D / RANK) * dot(orth[m], rj, 1, 0, HIGH)
-            update[m, :, cols] = out.astype(jnp.bfloat16)
+            out = math.sqrt(D / RANK) * dot(orth[m], right[m, :, cols], 1, 0, HIGH)
+            upd[m, :, cols] = out.astype(jnp.bfloat16)
             return carry
 
         lax.fori_loop(0, 4, direction, 0)
+        store(upd.at[m], update.at[m])
+    for cp in stores:
+        cp.wait()
     pc.drain()
 
 
-def place_kernel(update, momentum_next, basis_next, update_out, momentum_out, basis_out, sem):
-    pairs = [(basis_next.at[m], basis_out.at[m]) for m in range(2)]
+def place_kernel(update, momentum_next, basis_next, update_out, momentum_out, basis_out, uv, mv, bv, sem):
+    parts = [(basis_next, bv, basis_out, pl.ds(0, 16))]
+    for i in range(2):
+        parts.append((momentum_next, mv, momentum_out, pl.ds(128 * i, 128)))
+        parts.append((update, uv, update_out, pl.ds(128 * i, 128)))
+    loads, stores = [], []
     for m in range(2):
-        for i in range(2):
-            rows = pl.ds(128 * i, 128)
-            pairs.append((momentum_next.at[m, rows], momentum_out.at[m, rows]))
-            pairs.append((update.at[m, rows], update_out.at[m, rows]))
-    copies = [pltpu.make_async_copy(a, b, sem.at[i]) for i, (a, b) in enumerate(pairs)]
-    for cp in copies:
+        for src, held, dst, rows in parts:
+            i = len(loads)
+            loads.append(pltpu.make_async_copy(src.at[m, rows], held.at[m, rows], sem.at[2 * i]))
+            stores.append(pltpu.make_async_copy(held.at[m, rows], dst.at[m, rows], sem.at[2 * i + 1]))
+    for cp in loads:
         cp.start()
-    for cp in copies:
+    for a, b in zip(loads, stores):
+        a.wait()
+        b.start()
+    for cp in stores:
         cp.wait()
 
 
 def shards(gradient, momentum, right_basis):
     vmem = pl.BlockSpec(memory_space=pltpu.VMEM)
+    anywhere = pl.BlockSpec(memory_space=pl.ANY)
     shape = lambda s: jax.ShapeDtypeStruct(s, F32)
     buf = lambda *s: pltpu.VMEM(s, F32)
-    n = 126
+    half = pltpu.VMEM((2, 256, 1024), jnp.bfloat16)
+    out_shape = (jax.ShapeDtypeStruct((2, 256, 1024), jnp.bfloat16), shape((2, 256, 1024)), shape((2, 16, 1024)))
+    n = 200
     results = pl.pallas_call(
         kernel,
-        out_shape=(
-            jax.ShapeDtypeStruct((2, 256, 1024), jnp.bfloat16), shape((2, 256, 1024)), shape((2, 16, 1024))
-        ),
-        in_specs=[vmem] * 3,
-        out_specs=[vmem] * 3,
+        out_shape=out_shape,
+        in_specs=[anywhere, anywhere, vmem],
+        out_specs=[anywhere] * 3,
         scratch_shapes=[
+            half, buf(2, 256, 1024), half, buf(2, 16, 1024),
             buf(2, 256, 1024), buf(256, 1024), buf(4, 4, 2, 16, 1024),
-            buf(4, 8, 64, 128), buf(7, 4, 64, 128), buf(8, 64, RANK), buf(RANK, RANK),
+            buf(4, 8, 64, 128), buf(7, 4, 64, 128), buf(2, 8, 64, 256), buf(RANK, RANK),
             buf(4, 4, 2, 40, 128), buf(2, 3, 4, 40, 128), buf(2, 4, 40, 128), buf(2, 3, 40, 128),
-            buf(8, 2, 40, 128), buf(4, 4, 2, 40, 128),
-            buf(4, 4, 2, 16, 1024), buf(2, 3, 4, 16, 1024), buf(2, 4, 16, 1024), buf(2, 3, 16, 1024),
-            buf(2, 4, 4, 2, 16, 1024), buf(2, 4, 64, RANK),
+            buf(8, 16, 128), buf(7, 16, 128), buf(8, 16, 128), buf(4, 4, 2, 40, 128),
+            buf(2, 4, 4, 2, 8, 1024), buf(2, 2, 3, 4, 8, 1024), buf(2, 2, 4, 8, 1024), buf(2, 2, 3, 8, 1024),
+            buf(2, 2, 4, 4, 2, 8, 1024), buf(2, 2, 4, 64, 256),
             buf(10, 128, 128), buf(6, 128, 128), buf(2, RANK, RANK),
             buf(2, RANK, 1024), buf(2, 256, RANK), buf(2, 8, RANK), buf(8, 8, 128),
-            pltpu.SemaphoreType.DMA((n,)), pltpu.SemaphoreType.DMA((n,)),
+            pltpu.SemaphoreType.DMA((n,)), pltpu.SemaphoreType.DMA((n,)), pltpu.SemaphoreType.DMA((10,)),
         ],
         compiler_params=pltpu.CompilerParams(
             collective_id=0, has_side_effects=True, vmem_limit_bytes=VMEM_BYTES
         ),
         name="dion",
     )(gradient, momentum, right_basis)
-    anywhere = pl.BlockSpec(memory_space=pl.ANY)
     return pl.pallas_call(
         place_kernel,
-        out_shape=tuple(jax.ShapeDtypeStruct(r.shape, r.dtype) for r in results),
+        out_shape=out_shape,
         in_specs=[anywhere] * 3,
         out_specs=[anywhere] * 3,
-        scratch_shapes=[pltpu.SemaphoreType.DMA((10,))],
-        compiler_params=pltpu.CompilerParams(has_side_effects=True),
+        scratch_shapes=[half, buf(2, 256, 1024), buf(2, 16, 1024), pltpu.SemaphoreType.DMA((20,))],
+        compiler_params=pltpu.CompilerParams(vmem_limit_bytes=VMEM_BYTES),
         name="place",
     )(*results)
 

time: 236 us -> 136 us (0.58)
  Pallas kernels: 236 us -> 135 us
    pallas_call x2, Pallas kernels: 236 us -> 135 us  [the longest x1 132 us: shards(): pl.pallas_call(kernel, out_shape=out_shape, in_specs=[anywhere, anywhere,...]
where the time goes in v4:
time: 136 us
  Pallas kernels  135 us (99%)
    pallas_call x1, Pallas kernels, shards(): pl.pallas_call(kernel, out_shape=out_shape, in_specs=[anywhere, anywhere,...  132 us
    pallas_call x1, Pallas kernels, shards(): pl.pallas_call(place_kernel, out_shape=out_shape, in_specs=[anywhere] * 3...  2.93 us

profile of v4, /device:TPU:1, one launch (start us, length us, event | category | flops | bytes accessed | tf_op | source)
XLA Modules:
  0.0 136.0 jit_solution(7636140087970557099)
XLA Ops:
  0.6 132.3 %dion.1 = (bf16[2,256,1024]{2,1,0:T(8,128)(2,1)}, f32[2,256,1024]{2,1,0:T(8,128)}, f32[2,16,1024]{2,1,0:T(8,128)}) custom-call(bf16[2,256,1024]{2,1,0:T(8,128)(2,1)} %grad.1, f32[2,256,1024]{2,1,0:T(8,128)} %mom.1, f32[2,16,1024]{2,1,0:T(8,128)} %rb.1), custom_call_target="tpu_custom_call" | custom-call | tf_op jit(solution)/shard_map/dion/pallas_call | solution.py:571
  132.9 2.9 %place.1 = (bf16[2,256,1024]{2,1,0:T(8,128)(2,1)}, f32[2,256,1024]{2,1,0:T(8,128)}, f32[2,16,1024]{2,1,0:T(8,128)}) custom-call(bf16[2,256,1024]{2,1,0:T(8,128)(2,1)} %get-tuple-element.6.update, f32[2,256,1024]{2,1,0:T(8,128)} %get-tuple-element.7.momentum_next, f32[2,16,1024]{2,1,0:T(8,128)} %get-tuple-element.8.basis_next), custom_call_target="tpu_custom_call" | custom-call | tf_op jit(solution)/shard_map/place/pallas_call | solution.py:593

commit v5 on v4

--- a/solution.py
+++ b/solution.py
@@ -99,7 +99,7 @@
     def first(self):
         pc, buf = self.pc, self.buf
         self.one = []
-        for d in (1, 3, 2):
+        for d in (2, 1, 3):
             a, b = buf.at[pc.y, pc.x, 0], buf.at[pc.y, pc.x, 1]
             self.one.append(pc.copy(a, a, pc.dev(x=pc.xs(d))))
             self.one.append(pc.copy(b, b, pc.dev(y=pc.ys(d))))
@@ -107,34 +107,53 @@
     def second(self):
         pc, buf = self.pc, self.buf
         received(self.one)
-        self.two = {}
-        for d in (1, 3, 2):
+        self.two, self.passed = {}, []
+        for d in (1, 3):
             a, b = buf.at[pc.y, :, 0], buf.at[:, pc.x, 1]
             self.two[d] = (pc.copy(a, a, pc.dev(y=pc.ys(d))), pc.copy(b, b, pc.dev(x=pc.xs(d))))
 
+    def relay(self, d):
+        pc, buf = self.pc, self.buf
+        received(self.two[d])
+        half = pl.ds(0, 2) if d == 1 else pl.ds(2, 2)
+        a, b = buf.at[pc.ys(4 - d), half, 0], buf.at[half, pc.xs(4 - d), 1]
+        self.passed.append(pc.copy(a, a, pc.dev(y=pc.ys(d))))
+        self.passed.append(pc.copy(b, b, pc.dev(x=pc.xs(d))))
+
     def finish(self):
-        for d in (1, 3, 2):
-            received(self.two[d])
+        received(self.passed)
 
 
 class Scatter:
-    def __init__(self, pc, buf, r1, acc, r2):
-        self.pc, self.buf, self.r1, self.acc, self.r2 = pc, buf, r1, acc, r2
+    def __init__(self, pc, buf, rel, r1, acc, r2):
+        self.pc, self.buf, self.rel, self.r1, self.acc, self.r2 = pc, buf, rel, r1, acc, r2
 
     def first(self):
-        pc, buf = self.pc, self.buf
+        pc, buf, rel = self.pc, self.buf, self.rel
+        self.halves = []
+        for i, d in enumerate((1, 3)):
+            half = pl.ds(2 * i, 2)
+            self.halves.append(pc.copy(buf.at[pc.ys(2), half, 0], rel.at[0, i], pc.dev(y=pc.ys(d))))
+            self.halves.append(pc.copy(buf.at[half, pc.xs(2), 1], rel.at[1, i], pc.dev(x=pc.xs(d))))
+
+    def middle(self):
+        pc, buf, rel, r1 = self.pc, self.buf, self.rel, self.r1
+        received(self.halves)
         self.one = []
-        for d in (1, 3, 2):
-            self.one.append(pc.copy(buf.at[pc.ys(d), :, 0], self.r1.at[0, d - 1], pc.dev(y=pc.ys(d))))
-            self.one.append(pc.copy(buf.at[:, pc.xs(d), 1], self.r1.at[1, d - 1], pc.dev(x=pc.xs(d))))
+        for i, d in enumerate((1, 3)):
+            half = pl.ds(2 * i, 2)
+            buf[pc.ys(d), half, 0] = buf[pc.ys(d), half, 0] + rel[0, i]
+            self.one.append(pc.copy(buf.at[pc.ys(d), :, 0], r1.at[0, i], pc.dev(y=pc.ys(d))))
+            buf[half, pc.xs(d), 1] = buf[half, pc.xs(d), 1] + rel[1, i]
+            self.one.append(pc.copy(buf.at[:, pc.xs(d), 1], r1.at[1, i], pc.dev(x=pc.xs(d))))
 
     def second(self):
         pc, buf, r1, acc = self.pc, self.buf, self.r1, self.acc
         received(self.one)
-        acc[0] = buf[pc.y, :, 0] + r1[0, 0] + r1[0, 1] + r1[0, 2]
-        acc[1] = buf[:, pc.x, 1] + r1[1, 0] + r1[1, 1] + r1[1, 2]
+        acc[0] = buf[pc.y, :, 0] + r1[0, 0] + r1[0, 1]
+        acc[1] = buf[:, pc.x, 1] + r1[1, 0] + r1[1, 1]
         self.two = []
-        for d in (1, 3, 2):
+        for d in (2, 1, 3):
             self.two.append(pc.copy(acc.at[0, pc.xs(d)], self.r2.at[0, d - 1], pc.dev(x=pc.xs(d))))
             self.two.append(pc.copy(acc.at[1, pc.ys(d)], self.r2.at[1, d - 1], pc.dev(y=pc.ys(d))))
 
@@ -217,9 +236,9 @@
 
 def kernel(
     grad, mom, rb, update, momentum_next, basis_next,
-    gv, mv, upd, bnext, blend, blend_send, basis, lpart, lrecv, left, perm,
-    gbuf, gr1, gacc, gr2, zsrc, zpart, zfull, gfull,
-    wbuf, wr1, wacc, wr2, wall, left_all,
+    gv, mv, upd, bnext, blend, blend_send, basis, lpart, lrel, lrecv, left, perm,
+    gbuf, grel, gr1, gacc, gr2, zsrc, zpart, zfull, gfull,
+    wbuf, wrel, wr1, wacc, wr2, wall, left_all,
     work, ybuf, tri, right, orth, sums, squares,
     send_sem, recv_sem, local_sem,
 ):
@@ -278,22 +297,45 @@
     rank = ((py * 4 + px) * 2 + half) * 16 + low
     perm[...] = jnp.where(lax.broadcasted_iota(jnp.int32, (RANK, RANK), 1) == rank, 1.0, 0.0)
     blend_swap.wait_recv()
-    sums_in = []
+    sums_in, opposite = [], {}
+
+    def to_z(d, e):
+        i = e - 1 if e < 4 else e - 2
+        sums_in.append(pc.copy(lpart.at[d, pc.zs(e)], lrecv.at[i, d], pc.dev(z=pc.zs(e))))
+
+    def to_z_far(d):
+        received(opposite[d])
+        for i, e in enumerate((3, 5)):
+            rows = pl.ds(32 * i, 32)
+            lpart[d, pc.zs(e), rows] = lpart[d, pc.zs(e), rows] + lrel[i, d]
+            to_z(d, e)
+
+    before = None
     for d in (0, 3, 1, 2):
-        if d:
-            received(gather.two[4 - d])
+        if d == 2:
+            gather.finish()
+        elif d:
+            gather.relay(4 - d)
         rows = jnp.concatenate(
             [basis[pc.ys(d), :, 0].reshape(64, 1024), basis[:, pc.xs(d), 1].reshape(64, 1024)], axis=0
         )
         part = dot(blend[...].reshape(512, 1024), rows, 1, 1, HIGH)
         lpart[d] = part.reshape(8, 64, 128)
-        for e in (4, 3, 5, 2, 6, 1, 7):
-            sums_in.append(pc.copy(lpart.at[d, pc.zs(e)], lrecv.at[e - 1, d], pc.dev(z=pc.zs(e))))
+        opposite[d] = []
+        for i, e in enumerate((1, 7)):
+            src = lpart.at[d, pc.zs(4), pl.ds(32 * i, 32)]
+            opposite[d].append(pc.copy(src, lrel.at[i, d], pc.dev(z=pc.zs(e))))
+        if before is not None:
+            to_z_far(before)
+        for e in (2, 6, 1, 7):
+            to_z(d, e)
+        before = d
+    to_z_far(before)
     received(sums_in)
     own = []
     for d in range(4):
         s = lpart[d, z]
-        for e in range(7):
+        for e in range(6):
             s = s + lrecv[e, d]
         own.append(s)
     own = dot(jnp.concatenate(own, axis=1), perm[...], 1, 0, HIGHEST)
@@ -315,9 +357,10 @@
         row = dot(own[:, 128 * i:128 * i + 128], own[:, :128 * i + 128], 0, 0, HIGHEST)
         blocks += [row[:, 128 * j:128 * j + 128] for j in range(i + 1)]
     gbuf[...] = jnp.concatenate(blocks, axis=0).reshape(4, 4, 2, 40, 128)
-    gscatter = Scatter(pc, gbuf, gr1, gacc, gr2)
+    gscatter = Scatter(pc, gbuf, grel, gr1, gacc, gr2)
     gscatter.first()
     lefts = ring(1)
+    gscatter.middle()
     gscatter.second()
     received(lefts)
     lefts = ring(2)
@@ -351,8 +394,11 @@
             lt = left[q, :, :, 128 * i:128 * i + 128].reshape(RANK, 128)
             part = dot(lt, blend[...].reshape(512, 1024), 0, 0, HIGH)
             wbuf[q, 2 * i:2 * i + 2] = part.reshape(2, 4, 2, 8, 1024)
-        wscatter.append(Scatter(pc, wbuf.at[q], wr1.at[q], wacc.at[q], wr2.at[q]))
+        wscatter.append(Scatter(pc, wbuf.at[q], wrel.at[q], wr1.at[q], wacc.at[q], wr2.at[q]))
         wscatter[q].first()
+        if q == 0:
+            ggather.relay(1)
+            ggather.relay(3)
         wgather.append(Gather(pc, wall.at[c, q]))
     left_all[c] = left[:, pl.ds(4 * c, 4)]
     left_swap = pc.copy(left.at[:, pl.ds(4 * (1 - c), 4)], left_all.at[c], pc.partner())
@@ -371,27 +417,71 @@
         for a in (wall.at[c, q, y, :, 0], wall.at[c, q, :, x, 1]):
             w_swaps[q].append(pc.copy(a, a, pc.partner()))
 
+    def w_swap(q, parts):
+        for a in parts:
+            w_swaps[q].append(pc.copy(a, a, pc.partner()))
+
+    def w_relay(q):
+        for d in (1, 3):
+            wgather[q].relay(d)
+            w_swap(q, (wall.at[c, q, pc.ys(4 - d), :, 0], wall.at[c, q, :, pc.xs(4 - d), 1]))
+
     def w_last(q):
-        for d in (1, 3, 2):
-            received(wgather[q].two[d])
-            for a in (wall.at[c, q, pc.ys(4 - d), :, 0], wall.at[c, q, :, pc.xs(4 - d), 1]):
-                w_swaps[q].append(pc.copy(a, a, pc.partner()))
+        wgather[q].finish()
+        w_swap(q, (wall.at[c, q, pc.ys(2), :, 0], wall.at[c, q, :, pc.xs(2), 1]))
 
     def w_step1():
+        wscatter[0].middle()
+        wscatter[1].middle()
+
+    def w_step2():
         wscatter[0].second()
 
-    def w_step2():
+    def w_step3():
         wscatter[1].second()
         w_gather(0)
 
-    def w_step3():
+    def w_step4():
         w_gather(1)
         w_gather_second(0)
 
-    def w_step4():
+    def w_step5():
         w_gather_second(1)
-
-    events = {(1, 2): w_step1, (1, 28): w_step2, (2, 10): w_step3, (2, 26): w_step4}
+        w_relay(0)
+
+    def w_step6():
+        w_relay(1)
+
+    def w_step7():
+        w_last(0)
+
+    def w_step8():
+        w_last(1)
+
+    def raw_job(m, i, j):
+        def job():
+            cols = pl.ds(256 * j, 256)
+            n = 128 * (i + 1)
+            wj = [wall[m, q, :, :, :, :, cols].reshape(256, 256) for q in range(2 if i > 1 else 1)]
+            wj = jnp.concatenate(wj, axis=0)[:n]
+            t = tri[m, pl.ds(128 * i, 128), pl.ds(0, n)]
+            right[m, pl.ds(128 * i, 128), cols] = dot(t, wj, 1, 0, HIGH)
+
+        return job
+
+    def raw_own():
+        pending.extend(raw_job(c, i, j) for j in range(4) for i in range(3))
+
+    def raw_other():
+        received(tri_swaps)
+        received(w_swaps[0] + w_swaps[1])
+        tri_swaps.clear()
+        pending.extend(raw_job(1 - c, i, j) for j in range(4) for i in range(3))
+
+    events = {
+        (0, 8): w_step1, (0, 28): w_step2, (1, 6): w_step3, (1, 20): w_step4, (2, 4): w_step5, (2, 16): w_step6,
+        (2, 24): w_step7, (3, 0): w_step8, (3, 4): raw_own, (3, 17): raw_other,
+    }
     flat = gfull[...].reshape(1280, 128)
     for b in range(10):
         work[b] = flat[128 * b:128 * b + 128]
@@ -456,16 +546,11 @@
         else:
             tri_row(k, inv)
 
-    def raw(m, q):
+    def raw_end(m):
         def part(j, carry):
             cols = pl.ds(pl.multiple_of(j * 256, 256), 256)
-            wj = wall[m, q, :, :, :, :, cols].reshape(256, 256)
-            t = tri[m, pl.ds(256 * q, 512 - 256 * q), pl.ds(256 * q, 256)]
-            new = dot(t, wj, 1, 0, HIGH)
-            if q == 0:
-                right[m, :, cols] = new
-            else:
-                right[m, 256:, cols] = right[m, 256:, cols] + new
+            wj = wall[m, :, :, :, :, :, cols].reshape(RANK, 256)
+            right[m, 384:, cols] = dot(tri[m, 384:, :], wj, 1, 0, HIGH)
             return carry
 
         lax.fori_loop(0, 4, part, 0)
@@ -476,16 +561,10 @@
             fold = fold + right[m, :, 128 * j:128 * j + 128] * right[m, :, 128 * j:128 * j + 128]
         sums[m] = dot(jnp.ones((8, 128), F32), fold, 1, 1, HIGHEST)
 
-    w_last(0)
-    raw(c, 0)
-    w_last(1)
-    raw(c, 1)
+    raw_end(c)
     squares_of(c)
     received(tri_swaps)
-    received(w_swaps[0])
-    raw(1 - c, 0)
-    received(w_swaps[1])
-    raw(1 - c, 1)
+    raw_end(1 - c)
     squares_of(1 - c)
     left_swap.wait_recv()
     pieces = [sums[m, 0:1, 128 * j:128 * j + 128] for m in range(2) for j in range(4)]
@@ -567,7 +646,7 @@
     buf = lambda *s: pltpu.VMEM(s, F32)
     half = pltpu.VMEM((2, 256, 1024), jnp.bfloat16)
     out_shape = (jax.ShapeDtypeStruct((2, 256, 1024), jnp.bfloat16), shape((2, 256, 1024)), shape((2, 16, 1024)))
-    n = 200
+    n = 208
     results = pl.pallas_call(
         kernel,
         out_shape=out_shape,
@@ -576,10 +655,10 @@
         scratch_shapes=[
             half, buf(2, 256, 1024), half, buf(2, 16, 1024),
             buf(2, 256, 1024), buf(256, 1024), buf(4, 4, 2, 16, 1024),
-            buf(4, 8, 64, 128), buf(7, 4, 64, 128), buf(2, 8, 64, 256), buf(RANK, RANK),
-            buf(4, 4, 2, 40, 128), buf(2, 3, 4, 40, 128), buf(2, 4, 40, 128), buf(2, 3, 40, 128),
+            buf(4, 8, 64, 128), buf(2, 4, 32, 128), buf(6, 4, 64, 128), buf(2, 8, 64, 256), buf(RANK, RANK),
+            buf(4, 4, 2, 40, 128), buf(2, 2, 2, 40, 128), buf(2, 2, 4, 40, 128), buf(2, 4, 40, 128), buf(2, 3, 40, 128),
             buf(8, 16, 128), buf(7, 16, 128), buf(8, 16, 128), buf(4, 4, 2, 40, 128),
-            buf(2, 4, 4, 2, 8, 1024), buf(2, 2, 3, 4, 8, 1024), buf(2, 2, 4, 8, 1024), buf(2, 2, 3, 8, 1024),
+            buf(2, 4, 4, 2, 8, 1024), buf(2, 2, 2, 2, 8, 1024), buf(2, 2, 2, 4, 8, 1024), buf(2, 2, 4, 8, 1024), buf(2, 2, 3, 8, 1024),
             buf(2, 2, 4, 4, 2, 8, 1024), buf(2, 2, 4, 64, 256),
             buf(10, 128, 128), buf(6, 128, 128), buf(2, RANK, RANK),
             buf(2, RANK, 1024), buf(2, 256, RANK), buf(2, 8, RANK), buf(8, 8, 128),

time: 136 us -> 137 us (level)
  no operation moved by 1% of the time
where the time goes in v5:
time: 137 us
  Pallas kernels  136 us (99%)
    pallas_call x1, Pallas kernels, shards(): pl.pallas_call(kernel, out_shape=out_shape, in_specs=[anywhere, anywhere,...  133 us
    pallas_call x1, Pallas kernels, shards(): pl.pallas_call(place_kernel, out_shape=out_shape, in_specs=[anywhere] * 3...  2.93 us

profile of v5, /device:TPU:1, one launch (start us, length us, event | category | flops | bytes accessed | tf_op | source)
XLA Modules:
  0.0 137.1 jit_solution(4858602944088195565)
XLA Ops:
  0.6 133.3 %dion.1 = (bf16[2,256,1024]{2,1,0:T(8,128)(2,1)}, f32[2,256,1024]{2,1,0:T(8,128)}, f32[2,16,1024]{2,1,0:T(8,128)}) custom-call(bf16[2,256,1024]{2,1,0:T(8,128)(2,1)} %grad.1, f32[2,256,1024]{2,1,0:T(8,128)} %mom.1, f32[2,16,1024]{2,1,0:T(8,128)} %rb.1), custom_call_target="tpu_custom_call" | custom-call | tf_op jit(solution)/shard_map/dion/pallas_call | solution.py:650
  134.0 2.9 %place.1 = (bf16[2,256,1024]{2,1,0:T(8,128)(2,1)}, f32[2,256,1024]{2,1,0:T(8,128)}, f32[2,16,1024]{2,1,0:T(8,128)}) custom-call(bf16[2,256,1024]{2,1,0:T(8,128)(2,1)} %get-tuple-element.6.update, f32[2,256,1024]{2,1,0:T(8,128)} %get-tuple-element.7.momentum_next, f32[2,16,1024]{2,1,0:T(8,128)} %get-tuple-element.8.basis_next), custom_call_target="tpu_custom_call" | custom-call | tf_op jit(solution)/shard_map/place/pallas_call | solution.py:672

commit v6 on v5

--- a/solution.py
+++ b/solution.py
@@ -175,13 +175,18 @@
     def column(v, j):
         return jnp.broadcast_to(v[:, j:j + 1], (8, 128))
 
+    def spread(v, i):
+        return jnp.broadcast_to(v[i:i + 1, :], (8, 128))
+
     def recip(v):
         return pl.reciprocal(v, approx=True)
 
     for q in range(32):
         r0, s0, j0 = q // 2, 4 * (q % 2), 4 * q
-        rows = [jnp.broadcast_to(a[r0][s0 + s:s0 + s + 1, :], (8, 128)) for s in range(4)]
-        p = {(s, t): column(rows[s], j0 + t) for s in range(4) for t in range(s, 4)}
+        end = 4 * (r0 // 4) + 4
+        rows = [spread(a[r0], s0 + s) for s in range(4)]
+        cols = [column(a[r0], j0 + t) for t in range(4)]
+        p = {(s, t): spread(cols[t], s0 + s) for s in range(4) for t in range(s, 4)}
         inside = (lane >= j0) & (lane < j0 + 4)
         sc = [lax.rsqrt(p[s, s]) for s in range(4)]
         v = [jnp.where(inside, jnp.where(lane == j0 + s, 1.0, 0.0), rows[s]) * sc[s] for s in range(4)]
@@ -227,9 +232,20 @@
         for s in range(1, 4):
             o = jnp.where(sub == s0 + s, done[s], o)
         out[r0] = o if s0 == 0 else jnp.where(sub < 4, out[r0], o)
-        for g in range(r0 if s0 == 0 else r0 + 1, groups):
-            t = [column(a[g], j0 + t) * w[t] for t in range(4)]
+        for g in range(r0 if s0 == 0 else r0 + 1, end):
+            if g > r0:
+                cols = [column(a[g], j0 + t) for t in range(4)]
+            t = [cols[t] * w[t] for t in range(4)]
             a[g] = jnp.where(inside, 0.0, a[g]) - ((t[0] + t[1]) + (t[2] + t[3]))
+        if q % 8 == 7 and end < groups:
+            new = jnp.concatenate(out[end - 4:end], axis=0)
+            lanes = lax.broadcasted_iota(jnp.int32, (32, 128), 1)
+            over = lanes > 8 * end - 32 + lax.broadcasted_iota(jnp.int32, (32, 128), 0)
+            right = jnp.where(lanes >= 8 * end, new, 0.0)
+            step = dot(right, jnp.where(over, right, new), 0, 0, HIGHEST)
+            done_lanes = (lane >= 8 * end - 32) & (lane < 8 * end)
+            for g in range(end, groups):
+                a[g] = jnp.where(done_lanes, 0.0, a[g]) - step[8 * g:8 * g + 8]
         tick(q)
     return out
 

time: 137 us -> 137 us (level)
  no operation moved by 1% of the time
where the time goes in v6:
time: 137 us; the launch traced here: 136 us
  Pallas kernels  136 us (99%)
    pallas_call x1, Pallas kernels, shards(): pl.pallas_call(kernel, out_shape=out_shape, in_specs=[anywhere, anywhere,...  133 us
    pallas_call x1, Pallas kernels, shards(): pl.pallas_call(place_kernel, out_shape=out_shape, in_specs=[anywhere] * 3...  2.93 us

profile of v6, /device:TPU:1, one launch (start us, length us, event | category | flops | bytes accessed | tf_op | source)
XLA Modules:
  0.0 136.4 jit_solution(3048944701899084563)
XLA Ops:
  0.6 132.6 %dion.1 = (bf16[2,256,1024]{2,1,0:T(8,128)(2,1)}, f32[2,256,1024]{2,1,0:T(8,128)}, f32[2,16,1024]{2,1,0:T(8,128)}) custom-call(bf16[2,256,1024]{2,1,0:T(8,128)(2,1)} %grad.1, f32[2,256,1024]{2,1,0:T(8,128)} %mom.1, f32[2,16,1024]{2,1,0:T(8,128)} %rb.1), custom_call_target="tpu_custom_call" | custom-call | tf_op jit(solution)/shard_map/dion/pallas_call | solution.py:666
  133.3 2.9 %place.1 = (bf16[2,256,1024]{2,1,0:T(8,128)(2,1)}, f32[2,256,1024]{2,1,0:T(8,128)}, f32[2,16,1024]{2,1,0:T(8,128)}) custom-call(bf16[2,256,1024]{2,1,0:T(8,128)(2,1)} %get-tuple-element.6.update, f32[2,256,1024]{2,1,0:T(8,128)} %get-tuple-element.7.momentum_next, f32[2,16,1024]{2,1,0:T(8,128)} %get-tuple-element.8.basis_next), custom_call_target="tpu_custom_call" | custom-call | tf_op jit(solution)/shard_map/place/pallas_call | solution.py:688

commit v7 on v6

--- a/solution.py
+++ b/solution.py
@@ -81,10 +81,11 @@
             pl.semaphore_signal(sem, inc=1, device_id=p, device_id_type=MESH)
         pl.semaphore_wait(sem, len(peers))
 
-    def drain(self):
-        for cp in self.open:
+    def drain(self, keep=0):
+        n = len(self.open) - keep
+        for cp in self.open[:n]:
             cp.wait_send()
-        self.open = []
+        self.open = self.open[n:]
 
 
 def received(copies):
@@ -252,10 +253,10 @@
 
 def kernel(
     grad, mom, rb, update, momentum_next, basis_next,
-    gv, mv, upd, bnext, blend, blend_send, basis, lpart, lrel, lrecv, left, perm,
+    gv, mv, upd, usend, urecv, mrecv, bown, bsend, brecv, blend, blend_send, basis, lpart, lrel, lrecv, left, perm,
     gbuf, grel, gr1, gacc, gr2, zsrc, zpart, zfull, gfull,
-    wbuf, wrel, wr1, wacc, wr2, wall, left_all,
-    work, ybuf, tri, right, orth, sums, squares,
+    wbuf, wrel, wr1, wacc, wr2, wall,
+    work, ybuf, tri, right, orth, squares,
     send_sem, recv_sem, local_sem,
 ):
     pc = Place(send_sem, recv_sem)
@@ -415,36 +416,19 @@
         if q == 0:
             ggather.relay(1)
             ggather.relay(3)
-        wgather.append(Gather(pc, wall.at[c, q]))
-    left_all[c] = left[:, pl.ds(4 * c, 4)]
-    left_swap = pc.copy(left.at[:, pl.ds(4 * (1 - c), 4)], left_all.at[c], pc.partner())
+        wgather.append(Gather(pc, wall.at[q]))
+    pc.drain(keep=16)
     ggather.finish()
-
-    w_swaps = ([], [])
 
     def w_gather(q):
         o0, o1 = wscatter[q].finish()
-        wall[c, q, y, x, 0] = o0
-        wall[c, q, y, x, 1] = o1
+        wall[q, y, x, 0] = o0
+        wall[q, y, x, 1] = o1
         wgather[q].first()
 
-    def w_gather_second(q):
-        wgather[q].second()
-        for a in (wall.at[c, q, y, :, 0], wall.at[c, q, :, x, 1]):
-            w_swaps[q].append(pc.copy(a, a, pc.partner()))
-
-    def w_swap(q, parts):
-        for a in parts:
-            w_swaps[q].append(pc.copy(a, a, pc.partner()))
-
     def w_relay(q):
-        for d in (1, 3):
-            wgather[q].relay(d)
-            w_swap(q, (wall.at[c, q, pc.ys(4 - d), :, 0], wall.at[c, q, :, pc.xs(4 - d), 1]))
-
-    def w_last(q):
-        wgather[q].finish()
-        w_swap(q, (wall.at[c, q, pc.ys(2), :, 0], wall.at[c, q, :, pc.xs(2), 1]))
+        wgather[q].relay(1)
+        wgather[q].relay(3)
 
     def w_step1():
         wscatter[0].middle()
@@ -459,44 +443,52 @@
 
     def w_step4():
         w_gather(1)
-        w_gather_second(0)
+        wgather[0].second()
 
     def w_step5():
-        w_gather_second(1)
+        wgather[1].second()
         w_relay(0)
 
     def w_step6():
         w_relay(1)
 
     def w_step7():
-        w_last(0)
-
-    def w_step8():
-        w_last(1)
-
-    def raw_job(m, i, j):
+        wgather[0].finish()
+        wgather[1].finish()
+        pending.extend(raw_job(i, j) for j in range(4) for i in range(3))
+        pending.extend(feed_job(h, j) for j in range(4) for h in range(2))
+
+    def w_part(q, cols):
+        return wall[q, :, :, :, :, cols].reshape(256, 256)
+
+    def raw_job(i, j):
         def job():
             cols = pl.ds(256 * j, 256)
             n = 128 * (i + 1)
-            wj = [wall[m, q, :, :, :, :, cols].reshape(256, 256) for q in range(2 if i > 1 else 1)]
-            wj = jnp.concatenate(wj, axis=0)[:n]
-            t = tri[m, pl.ds(128 * i, 128), pl.ds(0, n)]
-            right[m, pl.ds(128 * i, 128), cols] = dot(t, wj, 1, 0, HIGH)
+            wj = jnp.concatenate([w_part(q, cols) for q in range(2 if i > 1 else 1)], axis=0)[:n]
+            right[128 * i:128 * i + 128, cols] = dot(tri[128 * i:128 * i + 128, 0:n], wj, 1, 0, HIGH)
 
         return job
 
-    def raw_own():
-        pending.extend(raw_job(c, i, j) for j in range(4) for i in range(3))
-
-    def raw_other():
-        received(tri_swaps)
-        received(w_swaps[0] + w_swaps[1])
-        tri_swaps.clear()
-        pending.extend(raw_job(1 - c, i, j) for j in range(4) for i in range(3))
+    def feed_job(h, j):
+        def job():
+            cols = pl.ds(256 * j, 256)
+            back = dot(orth[h, :, 0:384], right[0:384, cols], 1, 0, HIGH)
+            blend[h, :, cols] = blend[h, :, cols] - (1.0 - momentum_decay) * back
+
+        return job
+
+    def orth_job(k, h):
+        def job():
+            n = 128 * (k + 1)
+            rows = jnp.concatenate([left[q, 4 * h:4 * h + 4].reshape(256, 256) for q in range(2)], axis=1)[:, :n]
+            orth[h, :, 128 * k:n] = dot(rows, tri[128 * k:n, 0:n], 1, 1, HIGH)
+
+        return job
 
     events = {
         (0, 8): w_step1, (0, 28): w_step2, (1, 6): w_step3, (1, 20): w_step4, (2, 4): w_step5, (2, 16): w_step6,
-        (2, 24): w_step7, (3, 0): w_step8, (3, 4): raw_own, (3, 17): raw_other,
+        (3, 12): w_step7,
     }
     flat = gfull[...].reshape(1280, 128)
     for b in range(10):
@@ -505,20 +497,12 @@
     yat = lambda i, j: i * (i - 1) // 2 + j
     rowi = lax.broadcasted_iota(jnp.int32, (128, 128), 0)
     coli = lax.broadcasted_iota(jnp.int32, (128, 128), 1)
-    tri_swaps = []
     pending = []
 
     def tri_row(k, inv):
-        for j in range(4):
-            cols = pl.ds(128 * j, 128)
-            if j < k:
-                tri[c, pl.ds(128 * k, 128), cols] = dot(inv, ybuf[yat(k, j)], 1, 0, HIGHEST)
-            elif j == k:
-                tri[c, pl.ds(128 * k, 128), cols] = inv
-            else:
-                tri[c, pl.ds(128 * k, 128), cols] = jnp.zeros((128, 128), F32)
-        a = tri.at[c, pl.ds(128 * k, 128)]
-        tri_swaps.append(pc.copy(a, a, pc.partner()))
+        for j in range(k):
+            tri[128 * k:128 * k + 128, 128 * j:128 * j + 128] = dot(inv, ybuf[yat(k, j)], 1, 0, HIGHEST)
+        tri[128 * k:128 * k + 128, 128 * k:128 * k + 128] = inv
 
     def later(k, inv):
         def solve(i):
@@ -528,7 +512,7 @@
             work[at(i, j)] = work[at(i, j)] - dot(work[at(i, k)], work[at(j, k)], 1, 1, HIGHEST)
 
         def inverse(i, j):
-            new = dot(work[at(i, k)], tri[c, pl.ds(128 * k, 128), pl.ds(128 * j, 128)], 1, 0, HIGHEST)
+            new = dot(work[at(i, k)], tri[128 * k:128 * k + 128, 128 * j:128 * j + 128], 1, 0, HIGHEST)
             ybuf[yat(i, j)] = -new if j == k else ybuf[yat(i, j)] - new
 
         jobs = [lambda: tri_row(k, inv)]
@@ -540,7 +524,7 @@
         for i in range(k + 1, 4):
             for j in range(k + 1):
                 jobs.append(lambda i=i, j=j: inverse(i, j))
-        return jobs
+        return jobs + [orth_job(k, h) for h in range(2)]
 
     for k in range(4):
 
@@ -562,29 +546,25 @@
         else:
             tri_row(k, inv)
 
-    def raw_end(m):
-        def part(j, carry):
-            cols = pl.ds(pl.multiple_of(j * 256, 256), 256)
-            wj = wall[m, :, :, :, :, :, cols].reshape(RANK, 256)
-            right[m, 384:, cols] = dot(tri[m, 384:, :], wj, 1, 0, HIGH)
+
+    def columns(body):
+        def step(j, carry):
+            body(pl.ds(pl.multiple_of(j * 256, 256), 256))
             return carry
 
-        lax.fori_loop(0, 4, part, 0)
-
-    def squares_of(m):
-        fold = right[m, :, 0:128] * right[m, :, 0:128]
-        for j in range(1, 8):
-            fold = fold + right[m, :, 128 * j:128 * j + 128] * right[m, :, 128 * j:128 * j + 128]
-        sums[m] = dot(jnp.ones((8, 128), F32), fold, 1, 1, HIGHEST)
-
-    raw_end(c)
-    squares_of(c)
-    received(tri_swaps)
-    raw_end(1 - c)
-    squares_of(1 - c)
-    left_swap.wait_recv()
-    pieces = [sums[m, 0:1, 128 * j:128 * j + 128] for m in range(2) for j in range(4)]
-    squares[z] = jnp.concatenate(pieces, axis=0)
+        lax.fori_loop(0, 4, step, 0)
+
+    def raw_end(cols):
+        wj = jnp.concatenate([w_part(q, cols) for q in range(2)], axis=0)
+        new = dot(tri[384:, :], wj, 1, 0, HIGH)
+        right[384:, cols] = new
+
+    columns(raw_end)
+    fold = right[:, 0:128] * right[:, 0:128]
+    for j in range(1, 8):
+        fold = fold + right[:, 128 * j:128 * j + 128] * right[:, 128 * j:128 * j + 128]
+    sums = dot(jnp.ones((8, 128), F32), fold, 1, 1, HIGHEST)
+    squares[z] = jnp.concatenate([sums[0:1, 128 * j:128 * j + 128] for j in range(4)] * 2, axis=0)
     zs = []
     for d in (4, 3, 5, 2, 6, 1, 7):
         zs.append(pc.copy(squares.at[z], squares.at[z], pc.dev(z=pc.zs(d))))
@@ -595,41 +575,61 @@
         cp.start()
         stores.append(cp)
 
-    for m in range(2):
-        rows = jnp.concatenate([left_all[m, q].reshape(256, 256) for q in range(2)], axis=1)
-        orth[m] = dot(rows, tri[m], 1, 1, HIGH)
-
-        def feed(j, carry, m=m):
-            cols = pl.ds(pl.multiple_of(j * 256, 256), 256)
-            back = dot(orth[m], right[m, :, cols], 1, 0, HIGH)
-            blended = mv[m, :, cols] + gv[m, :, cols].astype(F32)
-            mv[m, :, cols] = blended - (1.0 - momentum_decay) * back
-            return carry
-
-        lax.fori_loop(0, 4, feed, 0)
-        store(mv.at[m], momentum_next.at[m])
+    for h in range(2):
+        orth_job(3, h)()
+
+    def feed(h):
+        def part(cols):
+            back = dot(orth[h, :, 384:], right[384:, cols], 1, 0, HIGH)
+            blend[h, :, cols] = blend[h, :, cols] - (1.0 - momentum_decay) * back
+
+        columns(part)
+
+    feed(1 - c)
+    momentum_swap = pc.copy(blend.at[1 - c], mrecv, pc.partner())
+    feed(c)
+    store(blend.at[c], momentum_next.at[c])
+    pc.drain(keep=8)
     received(zs)
     total = squares[0]
     for d in range(1, 8):
         total = total + squares[d]
     inverse = lax.rsqrt(total / D + epsilon_sq)
+    inv = jnp.concatenate([inverse[j:j + 1] for j in range(4)], axis=1)
     lane = lax.broadcasted_iota(jnp.int32, (16, RANK), 1)
     sub = lax.broadcasted_iota(jnp.int32, (16, RANK), 0)
-    for m in range(2):
-        inv = jnp.concatenate([inverse[4 * m + j:4 * m + j + 1] for j in range(4)], axis=1)
-        orth[m] = orth[m] * inv
-        pick = jnp.sum(jnp.where(lane == pc.f * 16 + sub, inv, 0.0), axis=1, keepdims=True)
-        bnext[m] = right[m, pl.ds(pl.multiple_of(pc.f * 16, 16), 16), :] * pick
-        store(bnext.at[m], basis_next.at[m])
-
-        def direction(j, carry, m=m):
-            cols = pl.ds(pl.multiple_of(j * 256, 256), 256)
-            out = math.sqrt(D / RANK) * dot(orth[m], right[m, :, cols], 1, 0, HIGH)
-            upd[m, :, cols] = out.astype(jnp.bfloat16)
-            return carry
-
-        lax.fori_loop(0, 4, direction, 0)
-        store(upd.at[m], update.at[m])
+
+    def basis_rows(f):
+        pick = jnp.sum(jnp.where(lane == f * 16 + sub, inv, 0.0), axis=1, keepdims=True)
+        return right[pl.ds(pl.multiple_of(f * 16, 16), 16), :] * pick
+
+    other = pc.f + 1 - 2 * c
+    bsend[...] = basis_rows(other)
+    basis_out_swap = pc.copy(bsend, brecv, pc.partner())
+    bown[...] = basis_rows(pc.f)
+    store(bown, basis_next.at[c])
+    for h in range(2):
+        orth[h] = orth[h] * (math.sqrt(D / RANK) * inv)
+    update_swaps = []
+    for i in range(2):
+        for j in range(2):
+            cols = pl.ds(512 * i + 256 * j, 256)
+            usend[i, :, 256 * j:256 * j + 256] = dot(orth[1 - c], right[:, cols], 1, 0, HIGH)
+        update_swaps.append(pc.copy(usend.at[i], urecv.at[i], pc.partner()))
+    momentum_swap.wait_recv()
+    store(mrecv, momentum_next.at[1 - c])
+
+    def direction(cols):
+        upd[c, :, cols] = dot(orth[c], right[:, cols], 1, 0, HIGH).astype(jnp.bfloat16)
+
+    columns(direction)
+    store(upd.at[c], update.at[c])
+    basis_out_swap.wait_recv()
+    store(brecv, basis_next.at[1 - c])
+    for i in range(2):
+        update_swaps[i].wait_recv()
+        upd[1 - c, :, 512 * i:512 * i + 512] = urecv[i].astype(jnp.bfloat16)
+    store(upd.at[1 - c], update.at[1 - c])
     for cp in stores:
         cp.wait()
     pc.drain()
@@ -669,15 +669,16 @@
         in_specs=[anywhere, anywhere, vmem],
         out_specs=[anywhere] * 3,
         scratch_shapes=[
-            half, buf(2, 256, 1024), half, buf(2, 16, 1024),
+            half, buf(2, 256, 1024), half, buf(2, 256, 512), buf(2, 256, 512), buf(256, 1024),
+            buf(16, 1024), buf(16, 1024), buf(16, 1024),
             buf(2, 256, 1024), buf(256, 1024), buf(4, 4, 2, 16, 1024),
             buf(4, 8, 64, 128), buf(2, 4, 32, 128), buf(6, 4, 64, 128), buf(2, 8, 64, 256), buf(RANK, RANK),
             buf(4, 4, 2, 40, 128), buf(2, 2, 2, 40, 128), buf(2, 2, 4, 40, 128), buf(2, 4, 40, 128), buf(2, 3, 40, 128),
             buf(8, 16, 128), buf(7, 16, 128), buf(8, 16, 128), buf(4, 4, 2, 40, 128),
             buf(2, 4, 4, 2, 8, 1024), buf(2, 2, 2, 2, 8, 1024), buf(2, 2, 2, 4, 8, 1024), buf(2, 2, 4, 8, 1024), buf(2, 2, 3, 8, 1024),
-            buf(2, 2, 4, 4, 2, 8, 1024), buf(2, 2, 4, 64, 256),
-            buf(10, 128, 128), buf(6, 128, 128), buf(2, RANK, RANK),
-            buf(2, RANK, 1024), buf(2, 256, RANK), buf(2, 8, RANK), buf(8, 8, 128),
+            buf(2, 4, 4, 2, 8, 1024),
+            buf(10, 128, 128), buf(6, 128, 128), buf(RANK, RANK),
+            buf(RANK, 1024), buf(2, 256, RANK), buf(8, 8, 128),
             pltpu.SemaphoreType.DMA((n,)), pltpu.SemaphoreType.DMA((n,)), pltpu.SemaphoreType.DMA((10,)),
         ],
         compiler_params=pltpu.CompilerParams(

time: 137 us -> 135 us (0.985)
  Pallas kernels: 136 us -> 134 us
    pallas_call x1, Pallas kernels: 133 us -> 131 us  [shards(): pl.pallas_call(kernel, out_shape=out_shape, in_specs=[anywhere, anywhere,...]
where the time goes in v7:
time: 135 us
  Pallas kernels  134 us (99%)
    pallas_call x1, Pallas kernels, shards(): pl.pallas_call(kernel, out_shape=out_shape, in_specs=[anywhere, anywhere,...  131 us
    pallas_call x1, Pallas kernels, shards(): pl.pallas_call(place_kernel, out_shape=out_shape, in_specs=[anywhere] * 3...  2.93 us

profile of v7, /device:TPU:1, one launch (start us, length us, event | category | flops | bytes accessed | tf_op | source)
XLA Modules:
  0.0 134.7 jit_solution(3734974149720242972)
XLA Ops:
  0.6 131.0 %dion.1 = (bf16[2,256,1024]{2,1,0:T(8,128)(2,1)}, f32[2,256,1024]{2,1,0:T(8,128)}, f32[2,16,1024]{2,1,0:T(8,128)}) custom-call(bf16[2,256,1024]{2,1,0:T(8,128)(2,1)} %grad.1, f32[2,256,1024]{2,1,0:T(8,128)} %mom.1, f32[2,16,1024]{2,1,0:T(8,128)} %rb.1), custom_call_target="tpu_custom_call" | custom-call | tf_op jit(solution)/shard_map/dion/pallas_call | solution.py:666
  131.6 2.9 %place.1 = (bf16[2,256,1024]{2,1,0:T(8,128)(2,1)}, f32[2,256,1024]{2,1,0:T(8,128)}, f32[2,16,1024]{2,1,0:T(8,128)}) custom-call(bf16[2,256,1024]{2,1,0:T(8,128)(2,1)} %get-tuple-element.6.update, f32[2,256,1024]{2,1,0:T(8,128)} %get-tuple-element.7.momentum_next, f32[2,16,1024]{2,1,0:T(8,128)} %get-tuple-element.8.basis_next), custom_call_target="tpu_custom_call" | custom-call | tf_op jit(solution)/shard_map/place/pallas_call | solution.py:689

commit v8 on v7

--- a/solution.py
+++ b/solution.py
@@ -12,6 +12,7 @@
 momentum_decay = 0.8
 epsilon_sq = 1e-06
 MESH = pl.DeviceIdType.MESH
+ALL = slice(None)
 F32 = jnp.float32
 HIGH = lax.Precision.HIGH
 HIGHEST = lax.Precision.HIGHEST
@@ -22,6 +23,37 @@
     return lax.dot_general(
         a, b, (((ca,), (cb,)), ((), ())), precision=precision, preferred_element_type=F32
     )
+
+
+class Loc:
+    def __init__(self, ref, *index):
+        self.ref, self.index = ref, index
+
+    def __call__(self):
+        return self.ref.at[self.index]
+
+
+class Copy:
+    def __init__(self, place, src, dst, send, recv, to):
+        self.place, self.src, self.dst, self.send, self.recv, self.to = place, src, dst, send, recv, to
+
+    def make(self):
+        src = self.src() if isinstance(self.src, Loc) else self.src
+        dst = self.dst() if isinstance(self.dst, Loc) else self.dst
+        return pltpu.make_async_remote_copy(
+            src_ref=src,
+            dst_ref=dst,
+            send_sem=self.place.send_sem.at[self.send],
+            recv_sem=self.place.recv_sem.at[self.recv],
+            device_id=self.to,
+            device_id_type=MESH,
+        )
+
+    def wait_send(self):
+        self.make().wait_send()
+
+    def wait_recv(self):
+        self.make().wait_recv()
 
 
 class Place:
@@ -32,6 +64,12 @@
         self.c = lax.rem(f, 2)
         self.x = lax.rem(f // 2, 4)
         self.y = f // 8
+        self.at_x = [lax.rem(self.x + d, 4) for d in range(4)]
+        self.at_y = [lax.rem(self.y + d, 4) for d in range(4)]
+        self.at_z = [lax.rem(self.z + d, 8) for d in range(8)]
+        self.to_x = [self.dev(x=v) for v in self.at_x]
+        self.to_y = [self.dev(y=v) for v in self.at_y]
+        self.to_z = [self.dev(z=v) for v in self.at_z]
         self.send_sem, self.recv_sem = send_sem, recv_sem
         self.count = 0
         self.open = []
@@ -47,13 +85,13 @@
         return self.dev(c=1 - self.c)
 
     def xs(self, d):
-        return lax.rem(self.x + d, 4)
+        return self.at_x[d]
 
     def ys(self, d):
-        return lax.rem(self.y + d, 4)
+        return self.at_y[d]
 
     def zs(self, d):
-        return lax.rem(self.z + d, 8)
+        return self.at_z[d % 8]
 
     def reserve(self, n):
         i = self.count
@@ -63,15 +101,8 @@
 
     def copy(self, src, dst, to, recv=None):
         i = self.reserve(1)
-        cp = pltpu.make_async_remote_copy(
-            src_ref=src,
-            dst_ref=dst,
-            send_sem=self.send_sem.at[i],
-            recv_sem=self.recv_sem.at[i if recv is None else recv],
-            device_id=to,
-            device_id_type=MESH,
-        )
-        cp.start()
+        cp = Copy(self, src, dst, i, i if recv is None else recv, to)
+        cp.make().start()
         self.open.append(cp)
         return cp
 
@@ -101,25 +132,25 @@
         pc, buf = self.pc, self.buf
         self.one = []
         for d in (2, 1, 3):
-            a, b = buf.at[pc.y, pc.x, 0], buf.at[pc.y, pc.x, 1]
-            self.one.append(pc.copy(a, a, pc.dev(x=pc.xs(d))))
-            self.one.append(pc.copy(b, b, pc.dev(y=pc.ys(d))))
+            a, b = Loc(buf, pc.y, pc.x, 0), Loc(buf, pc.y, pc.x, 1)
+            self.one.append(pc.copy(a, a, pc.to_x[d]))
+            self.one.append(pc.copy(b, b, pc.to_y[d]))
 
     def second(self):
         pc, buf = self.pc, self.buf
         received(self.one)
         self.two, self.passed = {}, []
         for d in (1, 3):
-            a, b = buf.at[pc.y, :, 0], buf.at[:, pc.x, 1]
-            self.two[d] = (pc.copy(a, a, pc.dev(y=pc.ys(d))), pc.copy(b, b, pc.dev(x=pc.xs(d))))
+            a, b = Loc(buf, pc.y, ALL, 0), Loc(buf, ALL, pc.x, 1)
+            self.two[d] = (pc.copy(a, a, pc.to_y[d]), pc.copy(b, b, pc.to_x[d]))
 
     def relay(self, d):
         pc, buf = self.pc, self.buf
         received(self.two[d])
         half = pl.ds(0, 2) if d == 1 else pl.ds(2, 2)
-        a, b = buf.at[pc.ys(4 - d), half, 0], buf.at[half, pc.xs(4 - d), 1]
-        self.passed.append(pc.copy(a, a, pc.dev(y=pc.ys(d))))
-        self.passed.append(pc.copy(b, b, pc.dev(x=pc.xs(d))))
+        a, b = Loc(buf, pc.ys(4 - d), half, 0), Loc(buf, half, pc.xs(4 - d), 1)
+        self.passed.append(pc.copy(a, a, pc.to_y[d]))
+        self.passed.append(pc.copy(b, b, pc.to_x[d]))
 
     def finish(self):
         received(self.passed)
@@ -134,8 +165,8 @@
         self.halves = []
         for i, d in enumerate((1, 3)):
             half = pl.ds(2 * i, 2)
-            self.halves.append(pc.copy(buf.at[pc.ys(2), half, 0], rel.at[0, i], pc.dev(y=pc.ys(d))))
-            self.halves.append(pc.copy(buf.at[half, pc.xs(2), 1], rel.at[1, i], pc.dev(x=pc.xs(d))))
+            self.halves.append(pc.copy(Loc(buf, pc.ys(2), half, 0), Loc(rel, 0, i), pc.to_y[d]))
+            self.halves.append(pc.copy(Loc(buf, half, pc.xs(2), 1), Loc(rel, 1, i), pc.to_x[d]))
 
     def middle(self):
         pc, buf, rel, r1 = self.pc, self.buf, self.rel, self.r1
@@ -144,9 +175,9 @@
         for i, d in enumerate((1, 3)):
             half = pl.ds(2 * i, 2)
             buf[pc.ys(d), half, 0] = buf[pc.ys(d), half, 0] + rel[0, i]
-            self.one.append(pc.copy(buf.at[pc.ys(d), :, 0], r1.at[0, i], pc.dev(y=pc.ys(d))))
+            self.one.append(pc.copy(Loc(buf, pc.ys(d), ALL, 0), Loc(r1, 0, i), pc.to_y[d]))
             buf[half, pc.xs(d), 1] = buf[half, pc.xs(d), 1] + rel[1, i]
-            self.one.append(pc.copy(buf.at[:, pc.xs(d), 1], r1.at[1, i], pc.dev(x=pc.xs(d))))
+            self.one.append(pc.copy(Loc(buf, ALL, pc.xs(d), 1), Loc(r1, 1, i), pc.to_x[d]))
 
     def second(self):
         pc, buf, r1, acc = self.pc, self.buf, self.r1, self.acc
@@ -155,8 +186,8 @@
         acc[1] = buf[:, pc.x, 1] + r1[1, 0] + r1[1, 1]
         self.two = []
         for d in (2, 1, 3):
-            self.two.append(pc.copy(acc.at[0, pc.xs(d)], self.r2.at[0, d - 1], pc.dev(x=pc.xs(d))))
-            self.two.append(pc.copy(acc.at[1, pc.ys(d)], self.r2.at[1, d - 1], pc.dev(y=pc.ys(d))))
+            self.two.append(pc.copy(Loc(acc, 0, pc.xs(d)), Loc(self.r2, 0, d - 1), pc.to_x[d]))
+            self.two.append(pc.copy(Loc(acc, 1, pc.ys(d)), Loc(self.r2, 1, d - 1), pc.to_y[d]))
 
     def finish(self):
         pc, acc, r2 = self.pc, self.acc, self.r2
@@ -166,12 +197,11 @@
         return own0, own1
 
 
-def factor_block(load, tick):
-    groups = 16
-    a = [load(r) for r in range(groups)]
+def factor_part(blk, b):
+    a = [blk[8 * g:8 * g + 8, :] for g in range(4)]
     lane = lax.broadcasted_iota(jnp.int32, (8, 128), 1)
     sub = lax.broadcasted_iota(jnp.int32, (8, 128), 0)
-    out = [None] * groups
+    out = [None] * 4
 
     def column(v, j):
         return jnp.broadcast_to(v[:, j:j + 1], (8, 128))
@@ -182,9 +212,8 @@
     def recip(v):
         return pl.reciprocal(v, approx=True)
 
-    for q in range(32):
+    for q in range(8):
         r0, s0, j0 = q // 2, 4 * (q % 2), 4 * q
-        end = 4 * (r0 // 4) + 4
         rows = [spread(a[r0], s0 + s) for s in range(4)]
         cols = [column(a[r0], j0 + t) for t in range(4)]
         p = {(s, t): spread(cols[t], s0 + s) for s in range(4) for t in range(s, 4)}
@@ -233,30 +262,28 @@
         for s in range(1, 4):
             o = jnp.where(sub == s0 + s, done[s], o)
         out[r0] = o if s0 == 0 else jnp.where(sub < 4, out[r0], o)
-        for g in range(r0 if s0 == 0 else r0 + 1, end):
+        for g in range(r0 if s0 == 0 else r0 + 1, 4):
             if g > r0:
                 cols = [column(a[g], j0 + t) for t in range(4)]
             t = [cols[t] * w[t] for t in range(4)]
             a[g] = jnp.where(inside, 0.0, a[g]) - ((t[0] + t[1]) + (t[2] + t[3]))
-        if q % 8 == 7 and end < groups:
-            new = jnp.concatenate(out[end - 4:end], axis=0)
-            lanes = lax.broadcasted_iota(jnp.int32, (32, 128), 1)
-            over = lanes > 8 * end - 32 + lax.broadcasted_iota(jnp.int32, (32, 128), 0)
-            right = jnp.where(lanes >= 8 * end, new, 0.0)
-            step = dot(right, jnp.where(over, right, new), 0, 0, HIGHEST)
-            done_lanes = (lane >= 8 * end - 32) & (lane < 8 * end)
-            for g in range(end, groups):
-                a[g] = jnp.where(done_lanes, 0.0, a[g]) - step[8 * g:8 * g + 8]
-        tick(q)
-    return out
+    new = jnp.concatenate(out, axis=0)
+    lanes = lax.broadcasted_iota(jnp.int32, (128, 128), 1)
+    rows = lax.broadcasted_iota(jnp.int32, (128, 128), 0)
+    live = 128 - 32 * b
+    below = jnp.where((lanes[:32] >= 32) & (lanes[:32] < live), new, 0.0)
+    step = dot(below, jnp.where((lanes[:32] > rows[:32]) & (lanes[:32] < live), below, new), 0, 0, HIGHEST)
+    rest = jnp.where((lanes[32:] < 32) & (rows[32:] < live), 0.0, blk[32:, :]) - step[32:]
+    blk[0:96, :] = pltpu.roll(rest, 96, 1)
+    blk[96:128, :] = pltpu.roll(new, 96, 1)
 
 
 def kernel(
     grad, mom, rb, update, momentum_next, basis_next,
-    gv, mv, upd, usend, urecv, mrecv, bown, bsend, brecv, blend, blend_send, basis, lpart, lrel, lrecv, left, perm,
+    gv, mv, upd, usend, urecv, mrecv, bown, bsend, brecv, blend, blend_send, basis, lpart, lrel, lrecv, left, leftt, ownp, perm,
     gbuf, grel, gr1, gacc, gr2, zsrc, zpart, zfull, gfull,
     wbuf, wrel, wr1, wacc, wr2, wall,
-    work, ybuf, tri, right, orth, squares,
+    work, ybuf, blk, tri, right, orth, squares,
     send_sem, recv_sem, local_sem,
 ):
     pc = Place(send_sem, recv_sem)
@@ -274,7 +301,7 @@
     peers = [pc.partner()]
     peers += [pc.dev(x=pc.xs(d), c=m) for d in (1, 2, 3) for m in (0, 1)]
     peers += [pc.dev(y=pc.ys(d), c=m) for d in (1, 2, 3) for m in (0, 1)]
-    peers += [pc.dev(z=pc.zs(d)) for d in range(1, 8)]
+    peers += [pc.to_z[d] for d in range(1, 8)]
     pc.barrier(peers)
 
     first = pc.reserve(6)
@@ -306,19 +333,25 @@
     gather = Gather(pc, basis)
     gather.one = []
     gather.second()
-    at = lax.broadcasted_iota(jnp.int32, (RANK, RANK), 0)
-    group, half = at // 128, (at // 64) % 2
-    index, low = (at // 16) % 4, at % 16
-    py = jnp.where(half == 0, (y + group) % 4, index)
-    px = jnp.where(half == 0, index, (x + group) % 4)
-    rank = ((py * 4 + px) * 2 + half) * 16 + low
-    perm[...] = jnp.where(lax.broadcasted_iota(jnp.int32, (RANK, RANK), 1) == rank, 1.0, 0.0)
+
+    def perm_part(i, carry):
+        at = lax.broadcasted_iota(jnp.int32, (64, RANK), 0)
+        group, half = i // 2, i % 2
+        index, low = at // 16, at % 16
+        py = (1 - half) * lax.rem(y + group, 4) + half * index
+        px = (1 - half) * index + half * lax.rem(x + group, 4)
+        rank = ((py * 4 + px) * 2 + half) * 16 + low
+        hit = lax.broadcasted_iota(jnp.int32, (64, RANK), 1) == rank
+        perm[pl.ds(pl.multiple_of(64 * i, 64), 64), :] = jnp.where(hit, 1.0, 0.0)
+        return carry
+
+    lax.fori_loop(0, 8, perm_part, 0)
     blend_swap.wait_recv()
     sums_in, opposite = [], {}
 
     def to_z(d, e):
         i = e - 1 if e < 4 else e - 2
-        sums_in.append(pc.copy(lpart.at[d, pc.zs(e)], lrecv.at[i, d], pc.dev(z=pc.zs(e))))
+        sums_in.append(pc.copy(lpart.at[d, pc.zs(e)], lrecv.at[i, d], pc.to_z[e]))
 
     def to_z_far(d):
         received(opposite[d])
@@ -333,15 +366,19 @@
             gather.finish()
         elif d:
             gather.relay(4 - d)
-        rows = jnp.concatenate(
-            [basis[pc.ys(d), :, 0].reshape(64, 1024), basis[:, pc.xs(d), 1].reshape(64, 1024)], axis=0
-        )
-        part = dot(blend[...].reshape(512, 1024), rows, 1, 1, HIGH)
-        lpart[d] = part.reshape(8, 64, 128)
+
+        def left_part(h, carry, d=d):
+            rows = jnp.concatenate(
+                [basis[pc.ys(d), :, 0].reshape(64, 1024), basis[:, pc.xs(d), 1].reshape(64, 1024)], axis=0
+            )
+            lpart[d, pl.ds(4 * h, 4)] = dot(blend[h], rows, 1, 1, HIGH).reshape(4, 64, 128)
+            return carry
+
+        lax.fori_loop(0, 2, left_part, 0)
         opposite[d] = []
         for i, e in enumerate((1, 7)):
             src = lpart.at[d, pc.zs(4), pl.ds(32 * i, 32)]
-            opposite[d].append(pc.copy(src, lrel.at[i, d], pc.dev(z=pc.zs(e))))
+            opposite[d].append(pc.copy(src, lrel.at[i, d], pc.to_z[e]))
         if before is not None:
             to_z_far(before)
         for e in (2, 6, 1, 7):
@@ -355,12 +392,19 @@
         for e in range(6):
             s = s + lrecv[e, d]
         own.append(s)
-    own = dot(jnp.concatenate(own, axis=1), perm[...], 1, 0, HIGHEST)
-    for q in range(2):
-        left[q, z] = own[:, 256 * q:256 * q + 256]
+    ownp[...] = jnp.concatenate(own, axis=1)
+
+    def order(j, carry):
+        cols = pl.ds(pl.multiple_of(128 * j, 128), 128)
+        own = dot(ownp[...], perm[:, cols], 1, 0, HIGHEST)
+        left[j // 2, z, :, pl.ds(pl.multiple_of(128 * (j % 2), 128), 128)] = own
+        return carry
+
+    lax.fori_loop(0, 4, order, 0)
+    own = jnp.concatenate([left[q, z] for q in range(2)], axis=1)
 
     def ring(step):
-        up, down = pc.dev(z=pc.zs(1)), pc.dev(z=pc.zs(7))
+        up, down = pc.to_z[1], pc.to_z[7]
         copies = []
         for q in range(2):
             a, b = left.at[q, pc.zs(9 - step)], left.at[q, pc.zs(step - 1)]
@@ -386,7 +430,7 @@
     zsrc[5:8] = jnp.zeros((3, 16, 128), F32)
     zs = []
     for d in (4, 3, 5, 2, 6, 1, 7):
-        zs.append(pc.copy(zsrc.at[pc.zs(d)], zpart.at[d - 1], pc.dev(z=pc.zs(d))))
+        zs.append(pc.copy(zsrc.at[pc.zs(d)], zpart.at[d - 1], pc.to_z[d]))
     received(lefts)
     lefts = ring(3)
     received(zs)
@@ -396,7 +440,7 @@
     zfull[z] = total
     zs = []
     for d in (4, 3, 5, 2, 6, 1, 7):
-        zs.append(pc.copy(zfull.at[z], zfull.at[z], pc.dev(z=pc.zs(d))))
+        zs.append(pc.copy(zfull.at[z], zfull.at[z], pc.to_z[d]))
     received(lefts)
     lefts = ring(4)
     received(zs)
@@ -408,9 +452,15 @@
     wscatter, wgather = [], []
     for q in range(2):
         for i in range(2):
-            lt = left[q, :, :, 128 * i:128 * i + 128].reshape(RANK, 128)
-            part = dot(lt, blend[...].reshape(512, 1024), 0, 0, HIGH)
-            wbuf[q, 2 * i:2 * i + 2] = part.reshape(2, 4, 2, 8, 1024)
+            leftt[256 * q + 128 * i:256 * q + 128 * i + 128, :] = left[q, :, :, 128 * i:128 * i + 128].reshape(RANK, 128).T
+
+        def w_product(j, carry, q=q):
+            cols = pl.ds(pl.multiple_of(256 * j, 256), 256)
+            part = dot(leftt[256 * q:256 * q + 256, :], blend[:, :, cols].reshape(512, 256), 1, 0, HIGH)
+            wbuf[q, :, :, :, :, cols] = part.reshape(4, 4, 2, 8, 256)
+            return carry
+
+        lax.fori_loop(0, 4, w_product, 0)
         wscatter.append(Scatter(pc, wbuf.at[q], wrel.at[q], wr1.at[q], wacc.at[q], wr2.at[q]))
         wscatter[q].first()
         if q == 0:
@@ -452,44 +502,10 @@
     def w_step6():
         w_relay(1)
 
-    def w_step7():
-        wgather[0].finish()
-        wgather[1].finish()
-        pending.extend(raw_job(i, j) for j in range(4) for i in range(3))
-        pending.extend(feed_job(h, j) for j in range(4) for h in range(2))
-
     def w_part(q, cols):
         return wall[q, :, :, :, :, cols].reshape(256, 256)
 
-    def raw_job(i, j):
-        def job():
-            cols = pl.ds(256 * j, 256)
-            n = 128 * (i + 1)
-            wj = jnp.concatenate([w_part(q, cols) for q in range(2 if i > 1 else 1)], axis=0)[:n]
-            right[128 * i:128 * i + 128, cols] = dot(tri[128 * i:128 * i + 128, 0:n], wj, 1, 0, HIGH)
-
-        return job
-
-    def feed_job(h, j):
-        def job():
-            cols = pl.ds(256 * j, 256)
-            back = dot(orth[h, :, 0:384], right[0:384, cols], 1, 0, HIGH)
-            blend[h, :, cols] = blend[h, :, cols] - (1.0 - momentum_decay) * back
-
-        return job
-
-    def orth_job(k, h):
-        def job():
-            n = 128 * (k + 1)
-            rows = jnp.concatenate([left[q, 4 * h:4 * h + 4].reshape(256, 256) for q in range(2)], axis=1)[:, :n]
-            orth[h, :, 128 * k:n] = dot(rows, tri[128 * k:n, 0:n], 1, 1, HIGH)
-
-        return job
-
-    events = {
-        (0, 8): w_step1, (0, 28): w_step2, (1, 6): w_step3, (1, 20): w_step4, (2, 4): w_step5, (2, 16): w_step6,
-        (3, 12): w_step7,
-    }
+    events = {1: w_step1, 3: w_step2, 5: w_step3, 7: w_step4, 9: w_step5, 11: w_step6}
     flat = gfull[...].reshape(1280, 128)
     for b in range(10):
         work[b] = flat[128 * b:128 * b + 128]
@@ -497,55 +513,40 @@
     yat = lambda i, j: i * (i - 1) // 2 + j
     rowi = lax.broadcasted_iota(jnp.int32, (128, 128), 0)
     coli = lax.broadcasted_iota(jnp.int32, (128, 128), 1)
-    pending = []
-
-    def tri_row(k, inv):
+    tri[...] = jnp.zeros((RANK, RANK), F32)
+
+    def panel_end(k):
+        inv = jnp.where(rowi >= coli, blk[...], 0.0)
+        tri[128 * k:128 * k + 128, 128 * k:128 * k + 128] = inv
+        for i in range(k + 1, 4):
+            work[at(i, k)] = dot(work[at(i, k)], inv, 1, 1, HIGHEST)
+        for i in range(k + 1, 4):
+            for j in range(k + 1, i + 1):
+                new = work[at(i, j)] - dot(work[at(i, k)], work[at(j, k)], 1, 1, HIGHEST)
+                work[at(i, j)] = new
+                if i == k + 1:
+                    blk[...] = new
         for j in range(k):
             tri[128 * k:128 * k + 128, 128 * j:128 * j + 128] = dot(inv, ybuf[yat(k, j)], 1, 0, HIGHEST)
-        tri[128 * k:128 * k + 128, 128 * k:128 * k + 128] = inv
-
-    def later(k, inv):
-        def solve(i):
-            work[at(i, k)] = dot(work[at(i, k)], inv, 1, 1, HIGHEST)
-
-        def trail(i, j):
-            work[at(i, j)] = work[at(i, j)] - dot(work[at(i, k)], work[at(j, k)], 1, 1, HIGHEST)
-
-        def inverse(i, j):
-            new = dot(work[at(i, k)], tri[128 * k:128 * k + 128, 128 * j:128 * j + 128], 1, 0, HIGHEST)
-            ybuf[yat(i, j)] = -new if j == k else ybuf[yat(i, j)] - new
-
-        jobs = [lambda: tri_row(k, inv)]
-        for i in range(k + 2, 4):
-            jobs.append(lambda i=i: solve(i))
-        for i in range(k + 2, 4):
-            for j in range(k + 1, i + 1):
-                jobs.append(lambda i=i, j=j: trail(i, j))
         for i in range(k + 1, 4):
             for j in range(k + 1):
-                jobs.append(lambda i=i, j=j: inverse(i, j))
-        return jobs + [orth_job(k, h) for h in range(2)]
-
-    for k in range(4):
-
-        def tick(q, k=k):
-            if (k, q) in events:
-                events[k, q]()
-            if pending and q >= 1:
-                pending.pop(0)()
-
-        rows = factor_block(lambda r: work[at(k, k), 8 * r:8 * r + 8, :], tick)
-        while pending:
-            pending.pop(0)()
-        inv = jnp.where(rowi >= coli, jnp.concatenate(rows, axis=0), 0.0)
-        if k < 3:
-            below = dot(work[at(k + 1, k)], inv, 1, 1, HIGHEST)
-            work[at(k + 1, k)] = below
-            work[at(k + 1, k + 1)] = work[at(k + 1, k + 1)] - dot(below, below, 1, 1, HIGHEST)
-            pending = later(k, inv)
-        else:
-            tri_row(k, inv)
-
+                new = dot(work[at(i, k)], tri[128 * k:128 * k + 128, 128 * j:128 * j + 128], 1, 0, HIGHEST)
+                ybuf[yat(i, j)] = -new if j == k else ybuf[yat(i, j)] - new
+
+    blk[...] = work[0]
+
+    def pivots(i, carry):
+        for n, event in events.items():
+            pl.when(i == n)(event)
+        factor_part(blk, lax.rem(i, 4))
+        for k in range(3):
+            pl.when(i == 4 * k + 3)(lambda k=k: panel_end(k))
+        return carry
+
+    lax.fori_loop(0, 16, pivots, 0)
+    panel_end(3)
+    wgather[0].finish()
+    wgather[1].finish()
 
     def columns(body):
         def step(j, carry):
@@ -556,8 +557,7 @@
 
     def raw_end(cols):
         wj = jnp.concatenate([w_part(q, cols) for q in range(2)], axis=0)
-        new = dot(tri[384:, :], wj, 1, 0, HIGH)
-        right[384:, cols] = new
+        right[:, cols] = dot(tri[...], wj, 1, 0, HIGH)
 
     columns(raw_end)
     fold = right[:, 0:128] * right[:, 0:128]
@@ -567,7 +567,7 @@
     squares[z] = jnp.concatenate([sums[0:1, 128 * j:128 * j + 128] for j in range(4)] * 2, axis=0)
     zs = []
     for d in (4, 3, 5, 2, 6, 1, 7):
-        zs.append(pc.copy(squares.at[z], squares.at[z], pc.dev(z=pc.zs(d))))
+        zs.append(pc.copy(squares.at[z], squares.at[z], pc.to_z[d]))
     stores = []
 
     def store(src, dst):
@@ -575,12 +575,16 @@
         cp.start()
         stores.append(cp)
 
-    for h in range(2):
-        orth_job(3, h)()
+    def orth_part(h, carry):
+        rows = jnp.concatenate([left[q, pl.ds(4 * h, 4)].reshape(256, 256) for q in range(2)], axis=1)
+        orth[h] = dot(rows, tri[...], 1, 1, HIGH)
+        return carry
+
+    lax.fori_loop(0, 2, orth_part, 0)
 
     def feed(h):
         def part(cols):
-            back = dot(orth[h, :, 384:], right[384:, cols], 1, 0, HIGH)
+            back = dot(orth[h], right[:, cols], 1, 0, HIGH)
             blend[h, :, cols] = blend[h, :, cols] - (1.0 - momentum_decay) * back
 
         columns(part)
@@ -612,9 +616,13 @@
         orth[h] = orth[h] * (math.sqrt(D / RANK) * inv)
     update_swaps = []
     for i in range(2):
-        for j in range(2):
-            cols = pl.ds(512 * i + 256 * j, 256)
-            usend[i, :, 256 * j:256 * j + 256] = dot(orth[1 - c], right[:, cols], 1, 0, HIGH)
+
+        def send_part(j, carry, i=i):
+            cols = pl.ds(pl.multiple_of(512 * i + 256 * j, 256), 256)
+            usend[i, :, pl.ds(pl.multiple_of(256 * j, 256), 256)] = dot(orth[1 - c], right[:, cols], 1, 0, HIGH)
+            return carry
+
+        lax.fori_loop(0, 2, send_part, 0)
         update_swaps.append(pc.copy(usend.at[i], urecv.at[i], pc.partner()))
     momentum_swap.wait_recv()
     store(mrecv, momentum_next.at[1 - c])
@@ -672,12 +680,12 @@
             half, buf(2, 256, 1024), half, buf(2, 256, 512), buf(2, 256, 512), buf(256, 1024),
             buf(16, 1024), buf(16, 1024), buf(16, 1024),
             buf(2, 256, 1024), buf(256, 1024), buf(4, 4, 2, 16, 1024),
-            buf(4, 8, 64, 128), buf(2, 4, 32, 128), buf(6, 4, 64, 128), buf(2, 8, 64, 256), buf(RANK, RANK),
+            buf(4, 8, 64, 128), buf(2, 4, 32, 128), buf(6, 4, 64, 128), buf(2, 8, 64, 256), buf(RANK, RANK), buf(64, RANK), buf(RANK, RANK),
             buf(4, 4, 2, 40, 128), buf(2, 2, 2, 40, 128), buf(2, 2, 4, 40, 128), buf(2, 4, 40, 128), buf(2, 3, 40, 128),
             buf(8, 16, 128), buf(7, 16, 128), buf(8, 16, 128), buf(4, 4, 2, 40, 128),
             buf(2, 4, 4, 2, 8, 1024), buf(2, 2, 2, 2, 8, 1024), buf(2, 2, 2, 4, 8, 1024), buf(2, 2, 4, 8, 1024), buf(2, 2, 3, 8, 1024),
             buf(2, 4, 4, 2, 8, 1024),
-            buf(10, 128, 128), buf(6, 128, 128), buf(RANK, RANK),
+            buf(10, 128, 128), buf(6, 128, 128), buf(128, 128), buf(RANK, RANK),
             buf(RANK, 1024), buf(2, 256, RANK), buf(8, 8, 128),
             pltpu.SemaphoreType.DMA((n,)), pltpu.SemaphoreType.DMA((n,)), pltpu.SemaphoreType.DMA((10,)),
         ],

time: 135 us -> 137 us (1.015)
  Pallas kernels: 134 us -> 136 us
    pallas_call x1, Pallas kernels: 131 us -> 133 us  [shards(): pl.pallas_call(kernel, out_shape=out_shape, in_specs=[anywhere, anywhere,...]
where the time goes in v8:
time: 137 us; the launch traced here: 136 us
  Pallas kernels  136 us (99%)
    pallas_call x1, Pallas kernels, shards(): pl.pallas_call(kernel, out_shape=out_shape, in_specs=[anywhere, anywhere,...  133 us
    pallas_call x1, Pallas kernels, shards(): pl.pallas_call(place_kernel, out_shape=out_shape, in_specs=[anywhere] * 3...  2.93 us

profile of v8, /device:TPU:1, one launch (start us, length us, event | category | flops | bytes accessed | tf_op | source)
XLA Modules:
  0.0 136.4 jit_solution(1784177322832514916)
XLA Ops:
  0.6 132.8 %dion.1 = (bf16[2,256,1024]{2,1,0:T(8,128)(2,1)}, f32[2,256,1024]{2,1,0:T(8,128)}, f32[2,16,1024]{2,1,0:T(8,128)}) custom-call(bf16[2,256,1024]{2,1,0:T(8,128)(2,1)} %grad.1, f32[2,256,1024]{2,1,0:T(8,128)} %mom.1, f32[2,16,1024]{2,1,0:T(8,128)} %rb.1), custom_call_target="tpu_custom_call" | custom-call | tf_op jit(solution)/shard_map/dion/pallas_call | solution.py:674
  133.5 2.9 %place.1 = (bf16[2,256,1024]{2,1,0:T(8,128)(2,1)}, f32[2,256,1024]{2,1,0:T(8,128)}, f32[2,16,1024]{2,1,0:T(8,128)}) custom-call(bf16[2,256,1024]{2,1,0:T(8,128)(2,1)} %get-tuple-element.6.update, f32[2,256,1024]{2,1,0:T(8,128)} %get-tuple-element.7.momentum_next, f32[2,16,1024]{2,1,0:T(8,128)} %get-tuple-element.8.basis_next), custom_call_target="tpu_custom_call" | custom-call | tf_op jit(solution)/shard_map/place/pallas_call | solution.py:697

commit v9 on v7

--- a/solution.py
+++ b/solution.py
@@ -100,7 +100,7 @@
     def first(self):
         pc, buf = self.pc, self.buf
         self.one = []
-        for d in (2, 1, 3):
+        for d in (1, 3, 2):
             a, b = buf.at[pc.y, pc.x, 0], buf.at[pc.y, pc.x, 1]
             self.one.append(pc.copy(a, a, pc.dev(x=pc.xs(d))))
             self.one.append(pc.copy(b, b, pc.dev(y=pc.ys(d))))
@@ -108,53 +108,34 @@
     def second(self):
         pc, buf = self.pc, self.buf
         received(self.one)
-        self.two, self.passed = {}, []
-        for d in (1, 3):
+        self.two = {}
+        for d in (1, 3, 2):
             a, b = buf.at[pc.y, :, 0], buf.at[:, pc.x, 1]
             self.two[d] = (pc.copy(a, a, pc.dev(y=pc.ys(d))), pc.copy(b, b, pc.dev(x=pc.xs(d))))
 
-    def relay(self, d):
+    def finish(self):
+        for d in (1, 3, 2):
+            received(self.two[d])
+
+
+class Scatter:
+    def __init__(self, pc, buf, r1, acc, r2):
+        self.pc, self.buf, self.r1, self.acc, self.r2 = pc, buf, r1, acc, r2
+
+    def first(self):
         pc, buf = self.pc, self.buf
-        received(self.two[d])
-        half = pl.ds(0, 2) if d == 1 else pl.ds(2, 2)
-        a, b = buf.at[pc.ys(4 - d), half, 0], buf.at[half, pc.xs(4 - d), 1]
-        self.passed.append(pc.copy(a, a, pc.dev(y=pc.ys(d))))
-        self.passed.append(pc.copy(b, b, pc.dev(x=pc.xs(d))))
-
-    def finish(self):
-        received(self.passed)
-
-
-class Scatter:
-    def __init__(self, pc, buf, rel, r1, acc, r2):
-        self.pc, self.buf, self.rel, self.r1, self.acc, self.r2 = pc, buf, rel, r1, acc, r2
-
-    def first(self):
-        pc, buf, rel = self.pc, self.buf, self.rel
-        self.halves = []
-        for i, d in enumerate((1, 3)):
-            half = pl.ds(2 * i, 2)
-            self.halves.append(pc.copy(buf.at[pc.ys(2), half, 0], rel.at[0, i], pc.dev(y=pc.ys(d))))
-            self.halves.append(pc.copy(buf.at[half, pc.xs(2), 1], rel.at[1, i], pc.dev(x=pc.xs(d))))
-
-    def middle(self):
-        pc, buf, rel, r1 = self.pc, self.buf, self.rel, self.r1
-        received(self.halves)
         self.one = []
-        for i, d in enumerate((1, 3)):
-            half = pl.ds(2 * i, 2)
-            buf[pc.ys(d), half, 0] = buf[pc.ys(d), half, 0] + rel[0, i]
-            self.one.append(pc.copy(buf.at[pc.ys(d), :, 0], r1.at[0, i], pc.dev(y=pc.ys(d))))
-            buf[half, pc.xs(d), 1] = buf[half, pc.xs(d), 1] + rel[1, i]
-            self.one.append(pc.copy(buf.at[:, pc.xs(d), 1], r1.at[1, i], pc.dev(x=pc.xs(d))))
+        for d in (1, 3, 2):
+            self.one.append(pc.copy(buf.at[pc.ys(d), :, 0], self.r1.at[0, d - 1], pc.dev(y=pc.ys(d))))
+            self.one.append(pc.copy(buf.at[:, pc.xs(d), 1], self.r1.at[1, d - 1], pc.dev(x=pc.xs(d))))
 
     def second(self):
         pc, buf, r1, acc = self.pc, self.buf, self.r1, self.acc
         received(self.one)
-        acc[0] = buf[pc.y, :, 0] + r1[0, 0] + r1[0, 1]
-        acc[1] = buf[:, pc.x, 1] + r1[1, 0] + r1[1, 1]
+        acc[0] = buf[pc.y, :, 0] + r1[0, 0] + r1[0, 1] + r1[0, 2]
+        acc[1] = buf[:, pc.x, 1] + r1[1, 0] + r1[1, 1] + r1[1, 2]
         self.two = []
-        for d in (2, 1, 3):
+        for d in (1, 3, 2):
             self.two.append(pc.copy(acc.at[0, pc.xs(d)], self.r2.at[0, d - 1], pc.dev(x=pc.xs(d))))
             self.two.append(pc.copy(acc.at[1, pc.ys(d)], self.r2.at[1, d - 1], pc.dev(y=pc.ys(d))))
 
@@ -253,9 +234,9 @@
 
 def kernel(
     grad, mom, rb, update, momentum_next, basis_next,
-    gv, mv, upd, usend, urecv, mrecv, bown, bsend, brecv, blend, blend_send, basis, lpart, lrel, lrecv, left, perm,
-    gbuf, grel, gr1, gacc, gr2, zsrc, zpart, zfull, gfull,
-    wbuf, wrel, wr1, wacc, wr2, wall,
+    gv, mv, upd, usend, urecv, mrecv, bown, bsend, brecv, blend, blend_send, basis, lpart, lrecv, left, perm,
+    gbuf, gr1, gacc, gr2, zsrc, zpart, zfull, gfull,
+    wbuf, wr1, wacc, wr2, wall,
     work, ybuf, tri, right, orth, squares,
     send_sem, recv_sem, local_sem,
 ):
@@ -312,50 +293,33 @@
     py = jnp.where(half == 0, (y + group) % 4, index)
     px = jnp.where(half == 0, index, (x + group) % 4)
     rank = ((py * 4 + px) * 2 + half) * 16 + low
-    perm[...] = jnp.where(lax.broadcasted_iota(jnp.int32, (RANK, RANK), 1) == rank, 1.0, 0.0)
+    perm[...] = jnp.where(lax.broadcasted_iota(jnp.int32, (RANK, RANK), 1) == rank, 1.0, 0.0).astype(jnp.bfloat16)
     blend_swap.wait_recv()
-    sums_in, opposite = [], {}
-
-    def to_z(d, e):
-        i = e - 1 if e < 4 else e - 2
-        sums_in.append(pc.copy(lpart.at[d, pc.zs(e)], lrecv.at[i, d], pc.dev(z=pc.zs(e))))
-
-    def to_z_far(d):
-        received(opposite[d])
-        for i, e in enumerate((3, 5)):
-            rows = pl.ds(32 * i, 32)
-            lpart[d, pc.zs(e), rows] = lpart[d, pc.zs(e), rows] + lrel[i, d]
-            to_z(d, e)
-
-    before = None
+    sums_in = []
     for d in (0, 3, 1, 2):
-        if d == 2:
-            gather.finish()
-        elif d:
-            gather.relay(4 - d)
+        if d:
+            received(gather.two[4 - d])
         rows = jnp.concatenate(
             [basis[pc.ys(d), :, 0].reshape(64, 1024), basis[:, pc.xs(d), 1].reshape(64, 1024)], axis=0
         )
         part = dot(blend[...].reshape(512, 1024), rows, 1, 1, HIGH)
         lpart[d] = part.reshape(8, 64, 128)
-        opposite[d] = []
-        for i, e in enumerate((1, 7)):
-            src = lpart.at[d, pc.zs(4), pl.ds(32 * i, 32)]
-            opposite[d].append(pc.copy(src, lrel.at[i, d], pc.dev(z=pc.zs(e))))
-        if before is not None:
-            to_z_far(before)
-        for e in (2, 6, 1, 7):
-            to_z(d, e)
-        before = d
-    to_z_far(before)
+        for e in (4, 3, 5, 2, 6, 1, 7):
+            sums_in.append(pc.copy(lpart.at[d, pc.zs(e)], lrecv.at[e - 1, d], pc.dev(z=pc.zs(e))))
     received(sums_in)
     own = []
     for d in range(4):
         s = lpart[d, z]
-        for e in range(6):
+        for e in range(7):
             s = s + lrecv[e, d]
         own.append(s)
-    own = dot(jnp.concatenate(own, axis=1), perm[...], 1, 0, HIGHEST)
+    own = jnp.concatenate(own, axis=1)
+    high = own.astype(jnp.bfloat16)
+    rest = own - high.astype(F32)
+    mid = rest.astype(jnp.bfloat16)
+    low = (rest - mid.astype(F32)).astype(jnp.bfloat16)
+    parts = dot(jnp.concatenate([high, mid, low], axis=0), perm[...], 1, 0, None)
+    own = (parts[0:64] + parts[64:128]) + parts[128:192]
     for q in range(2):
         left[q, z] = own[:, 256 * q:256 * q + 256]
 
@@ -374,10 +338,9 @@
         row = dot(own[:, 128 * i:128 * i + 128], own[:, :128 * i + 128], 0, 0, HIGHEST)
         blocks += [row[:, 128 * j:128 * j + 128] for j in range(i + 1)]
     gbuf[...] = jnp.concatenate(blocks, axis=0).reshape(4, 4, 2, 40, 128)
-    gscatter = Scatter(pc, gbuf, grel, gr1, gacc, gr2)
+    gscatter = Scatter(pc, gbuf, gr1, gacc, gr2)
     gscatter.first()
     lefts = ring(1)
-    gscatter.middle()
     gscatter.second()
     received(lefts)
     lefts = ring(2)
@@ -411,13 +374,10 @@
             lt = left[q, :, :, 128 * i:128 * i + 128].reshape(RANK, 128)
             part = dot(lt, blend[...].reshape(512, 1024), 0, 0, HIGH)
             wbuf[q, 2 * i:2 * i + 2] = part.reshape(2, 4, 2, 8, 1024)
-        wscatter.append(Scatter(pc, wbuf.at[q], wrel.at[q], wr1.at[q], wacc.at[q], wr2.at[q]))
+        wscatter.append(Scatter(pc, wbuf.at[q], wr1.at[q], wacc.at[q], wr2.at[q]))
         wscatter[q].first()
-        if q == 0:
-            ggather.relay(1)
-            ggather.relay(3)
         wgather.append(Gather(pc, wall.at[q]))
-    pc.drain(keep=16)
+    pc.drain(keep=18)
     ggather.finish()
 
     def w_gather(q):
@@ -426,33 +386,21 @@
         wall[q, y, x, 1] = o1
         wgather[q].first()
 
-    def w_relay(q):
-        wgather[q].relay(1)
-        wgather[q].relay(3)
-
     def w_step1():
-        wscatter[0].middle()
-        wscatter[1].middle()
+        wscatter[0].second()
 
     def w_step2():
-        wscatter[0].second()
-
-    def w_step3():
         wscatter[1].second()
         w_gather(0)
 
-    def w_step4():
+    def w_step3():
         w_gather(1)
         wgather[0].second()
 
-    def w_step5():
+    def w_step4():
         wgather[1].second()
-        w_relay(0)
-
-    def w_step6():
-        w_relay(1)
-
-    def w_step7():
+
+    def w_last():
         wgather[0].finish()
         wgather[1].finish()
         pending.extend(raw_job(i, j) for j in range(4) for i in range(3))
@@ -486,10 +434,7 @@
 
         return job
 
-    events = {
-        (0, 8): w_step1, (0, 28): w_step2, (1, 6): w_step3, (1, 20): w_step4, (2, 4): w_step5, (2, 16): w_step6,
-        (3, 12): w_step7,
-    }
+    events = {(0, 18): w_step1, (1, 4): w_step2, (1, 20): w_step3, (2, 6): w_step4, (3, 12): w_last}
     flat = gfull[...].reshape(1280, 128)
     for b in range(10):
         work[b] = flat[128 * b:128 * b + 128]
@@ -672,10 +617,10 @@
             half, buf(2, 256, 1024), half, buf(2, 256, 512), buf(2, 256, 512), buf(256, 1024),
             buf(16, 1024), buf(16, 1024), buf(16, 1024),
             buf(2, 256, 1024), buf(256, 1024), buf(4, 4, 2, 16, 1024),
-            buf(4, 8, 64, 128), buf(2, 4, 32, 128), buf(6, 4, 64, 128), buf(2, 8, 64, 256), buf(RANK, RANK),
-            buf(4, 4, 2, 40, 128), buf(2, 2, 2, 40, 128), buf(2, 2, 4, 40, 128), buf(2, 4, 40, 128), buf(2, 3, 40, 128),
+            buf(4, 8, 64, 128), buf(7, 4, 64, 128), buf(2, 8, 64, 256), pltpu.VMEM((RANK, RANK), jnp.bfloat16),
+            buf(4, 4, 2, 40, 128), buf(2, 3, 4, 40, 128), buf(2, 4, 40, 128), buf(2, 3, 40, 128),
             buf(8, 16, 128), buf(7, 16, 128), buf(8, 16, 128), buf(4, 4, 2, 40, 128),
-            buf(2, 4, 4, 2, 8, 1024), buf(2, 2, 2, 2, 8, 1024), buf(2, 2, 2, 4, 8, 1024), buf(2, 2, 4, 8, 1024), buf(2, 2, 3, 8, 1024),
+            buf(2, 4, 4, 2, 8, 1024), buf(2, 2, 3, 4, 8, 1024), buf(2, 2, 4, 8, 1024), buf(2, 2, 3, 8, 1024),
             buf(2, 4, 4, 2, 8, 1024),
             buf(10, 128, 128), buf(6, 128, 128), buf(RANK, RANK),
             buf(RANK, 1024), buf(2, 256, RANK), buf(8, 8, 128),

time: 135 us -> 133 us (0.985)
  Pallas kernels: 134 us -> 132 us
    pallas_call x1, Pallas kernels: 131 us -> 129 us  [shards(): pl.pallas_call(kernel, out_shape=out_shape, in_specs=[anywhere, anywhere,...]
where the time goes in v9:
time: 133 us
  Pallas kernels  132 us (99%)
    pallas_call x1, Pallas kernels, shards(): pl.pallas_call(kernel, out_shape=out_shape, in_specs=[anywhere, anywhere,...  129 us
    pallas_call x1, Pallas kernels, shards(): pl.pallas_call(place_kernel, out_shape=out_shape, in_specs=[anywhere] * 3...  2.93 us

profile of v9, /device:TPU:1, one launch (start us, length us, event | category | flops | bytes accessed | tf_op | source)
XLA Modules:
  0.0 132.9 jit_solution(12285978778491128711)
XLA Ops:
  0.6 129.2 %dion.1 = (bf16[2,256,1024]{2,1,0:T(8,128)(2,1)}, f32[2,256,1024]{2,1,0:T(8,128)}, f32[2,16,1024]{2,1,0:T(8,128)}) custom-call(bf16[2,256,1024]{2,1,0:T(8,128)(2,1)} %grad.1, f32[2,256,1024]{2,1,0:T(8,128)} %mom.1, f32[2,16,1024]{2,1,0:T(8,128)} %rb.1), custom_call_target="tpu_custom_call" | custom-call | tf_op jit(solution)/shard_map/dion/pallas_call | solution.py:611
  129.8 2.9 %place.1 = (bf16[2,256,1024]{2,1,0:T(8,128)(2,1)}, f32[2,256,1024]{2,1,0:T(8,128)}, f32[2,16,1024]{2,1,0:T(8,128)}) custom-call(bf16[2,256,1024]{2,1,0:T(8,128)(2,1)} %get-tuple-element.6.update, f32[2,256,1024]{2,1,0:T(8,128)} %get-tuple-element.7.momentum_next, f32[2,16,1024]{2,1,0:T(8,128)} %get-tuple-element.8.basis_next), custom_call_target="tpu_custom_call" | custom-call | tf_op jit(solution)/shard_map/place/pallas_call | solution.py:634

commit v10 on v9

--- a/solution.py
+++ b/solution.py
@@ -105,11 +105,14 @@
             self.one.append(pc.copy(a, a, pc.dev(x=pc.xs(d))))
             self.one.append(pc.copy(b, b, pc.dev(y=pc.ys(d))))
 
-    def second(self):
-        pc, buf = self.pc, self.buf
+    def second(self, ways=(1, 3, 2)):
         received(self.one)
         self.two = {}
-        for d in (1, 3, 2):
+        self.send_on(ways)
+
+    def send_on(self, ways):
+        pc, buf = self.pc, self.buf
+        for d in ways:
             a, b = buf.at[pc.y, :, 0], buf.at[:, pc.x, 1]
             self.two[d] = (pc.copy(a, a, pc.dev(y=pc.ys(d))), pc.copy(b, b, pc.dev(x=pc.xs(d))))
 
@@ -286,7 +289,7 @@
             ).wait_recv()
     gather = Gather(pc, basis)
     gather.one = []
-    gather.second()
+    gather.second((1, 3))
     at = lax.broadcasted_iota(jnp.int32, (RANK, RANK), 0)
     group, half = at // 128, (at // 64) % 2
     index, low = (at // 16) % 4, at % 16
@@ -299,6 +302,8 @@
     for d in (0, 3, 1, 2):
         if d:
             received(gather.two[4 - d])
+        if d == 3:
+            gather.send_on((2,))
         rows = jnp.concatenate(
             [basis[pc.ys(d), :, 0].reshape(64, 1024), basis[:, pc.xs(d), 1].reshape(64, 1024)], axis=0
         )

time: 133 us -> 128 us (0.962)
  Pallas kernels: 132 us -> 127 us
    pallas_call x1, Pallas kernels: 129 us -> 124 us  [shards(): pl.pallas_call(kernel, out_shape=out_shape, in_specs=[anywhere, anywhere,...]
where the time goes in v10:
time: 128 us
  Pallas kernels  127 us (99%)
    pallas_call x1, Pallas kernels, shards(): pl.pallas_call(kernel, out_shape=out_shape, in_specs=[anywhere, anywhere,...  124 us
    pallas_call x1, Pallas kernels, shards(): pl.pallas_call(place_kernel, out_shape=out_shape, in_specs=[anywhere] * 3...  2.93 us

profile of v10, /device:TPU:1, one launch (start us, length us, event | category | flops | bytes accessed | tf_op | source)
XLA Modules:
  0.0 128.0 jit_solution(5333876520150309094)
XLA Ops:
  0.6 124.2 %dion.1 = (bf16[2,256,1024]{2,1,0:T(8,128)(2,1)}, f32[2,256,1024]{2,1,0:T(8,128)}, f32[2,16,1024]{2,1,0:T(8,128)}) custom-call(bf16[2,256,1024]{2,1,0:T(8,128)(2,1)} %grad.1, f32[2,256,1024]{2,1,0:T(8,128)} %mom.1, f32[2,16,1024]{2,1,0:T(8,128)} %rb.1), custom_call_target="tpu_custom_call" | custom-call | tf_op jit(solution)/shard_map/dion/pallas_call | solution.py:616
  124.9 2.9 %place.1 = (bf16[2,256,1024]{2,1,0:T(8,128)(2,1)}, f32[2,256,1024]{2,1,0:T(8,128)}, f32[2,16,1024]{2,1,0:T(8,128)}) custom-call(bf16[2,256,1024]{2,1,0:T(8,128)(2,1)} %get-tuple-element.6.update, f32[2,256,1024]{2,1,0:T(8,128)} %get-tuple-element.7.momentum_next, f32[2,16,1024]{2,1,0:T(8,128)} %get-tuple-element.8.basis_next), custom_call_target="tpu_custom_call" | custom-call | tf_op jit(solution)/shard_map/place/pallas_call | solution.py:639

commit v11 on v10

--- a/solution.py
+++ b/solution.py
@@ -346,17 +346,15 @@
     gscatter = Scatter(pc, gbuf, gr1, gacc, gr2)
     gscatter.first()
     lefts = ring(1)
-    gscatter.second()
     received(lefts)
     lefts = ring(2)
+    gscatter.second()
     own0, own1 = gscatter.finish()
     zsrc[0:5] = jnp.concatenate([own0, own1], axis=0).reshape(5, 16, 128)
     zsrc[5:8] = jnp.zeros((3, 16, 128), F32)
     zs = []
     for d in (4, 3, 5, 2, 6, 1, 7):
         zs.append(pc.copy(zsrc.at[pc.zs(d)], zpart.at[d - 1], pc.dev(z=pc.zs(d))))
-    received(lefts)
-    lefts = ring(3)
     received(zs)
     total = zsrc[z]
     for d in range(7):
@@ -366,13 +364,15 @@
     for d in (4, 3, 5, 2, 6, 1, 7):
         zs.append(pc.copy(zfull.at[z], zfull.at[z], pc.dev(z=pc.zs(d))))
     received(lefts)
-    lefts = ring(4)
+    lefts = ring(3)
     received(zs)
     gfull[y, x] = zfull[0:5].reshape(2, 40, 128)
     ggather = Gather(pc, gfull)
     ggather.first()
     received(lefts)
+    lefts = ring(4)
     ggather.second()
+    received(lefts)
     wscatter, wgather = [], []
     for q in range(2):
         for i in range(2):
@@ -380,10 +380,11 @@
             part = dot(lt, blend[...].reshape(512, 1024), 0, 0, HIGH)
             wbuf[q, 2 * i:2 * i + 2] = part.reshape(2, 4, 2, 8, 1024)
         wscatter.append(Scatter(pc, wbuf.at[q], wr1.at[q], wacc.at[q], wr2.at[q]))
+        wgather.append(Gather(pc, wall.at[q]))
+    pc.drain(keep=6)
+    ggather.finish()
+    for q in range(2):
         wscatter[q].first()
-        wgather.append(Gather(pc, wall.at[q]))
-    pc.drain(keep=18)
-    ggather.finish()
 
     def w_gather(q):
         o0, o1 = wscatter[q].finish()
@@ -439,7 +440,7 @@
 
         return job
 
-    events = {(0, 18): w_step1, (1, 4): w_step2, (1, 20): w_step3, (2, 6): w_step4, (3, 12): w_last}
+    events = {(1, 0): w_step1, (1, 12): w_step2, (1, 26): w_step3, (2, 12): w_step4, (3, 12): w_last}
     flat = gfull[...].reshape(1280, 128)
     for b in range(10):
         work[b] = flat[128 * b:128 * b + 128]

time: 128 us -> 129 us (level)
  no operation moved by 1% of the time
where the time goes in v11:
time: 129 us
  Pallas kernels  128 us (99%)
    pallas_call x1, Pallas kernels, shards(): pl.pallas_call(kernel, out_shape=out_shape, in_specs=[anywhere, anywhere,...  125 us
    pallas_call x1, Pallas kernels, shards(): pl.pallas_call(place_kernel, out_shape=out_shape, in_specs=[anywhere] * 3...  2.93 us

profile of v11, /device:TPU:1, one launch (start us, length us, event | category | flops | bytes accessed | tf_op | source)
XLA Modules:
  0.0 128.8 jit_solution(10996260538704860010)
XLA Ops:
  0.6 125.1 %dion.1 = (bf16[2,256,1024]{2,1,0:T(8,128)(2,1)}, f32[2,256,1024]{2,1,0:T(8,128)}, f32[2,16,1024]{2,1,0:T(8,128)}) custom-call(bf16[2,256,1024]{2,1,0:T(8,128)(2,1)} %grad.1, f32[2,256,1024]{2,1,0:T(8,128)} %mom.1, f32[2,16,1024]{2,1,0:T(8,128)} %rb.1), custom_call_target="tpu_custom_call" | custom-call | tf_op jit(solution)/shard_map/dion/pallas_call | solution.py:617
  125.7 2.9 %place.1 = (bf16[2,256,1024]{2,1,0:T(8,128)(2,1)}, f32[2,256,1024]{2,1,0:T(8,128)}, f32[2,16,1024]{2,1,0:T(8,128)}) custom-call(bf16[2,256,1024]{2,1,0:T(8,128)(2,1)} %get-tuple-element.6.update, f32[2,256,1024]{2,1,0:T(8,128)} %get-tuple-element.7.momentum_next, f32[2,16,1024]{2,1,0:T(8,128)} %get-tuple-element.8.basis_next), custom_call_target="tpu_custom_call" | custom-call | tf_op jit(solution)/shard_map/place/pallas_call | solution.py:640

commit v12 on v10

--- a/solution.py
+++ b/solution.py
@@ -346,9 +346,9 @@
     gscatter = Scatter(pc, gbuf, gr1, gacc, gr2)
     gscatter.first()
     lefts = ring(1)
-    gscatter.second()
     received(lefts)
     lefts = ring(2)
+    gscatter.second()
     own0, own1 = gscatter.finish()
     zsrc[0:5] = jnp.concatenate([own0, own1], axis=0).reshape(5, 16, 128)
     zsrc[5:8] = jnp.zeros((3, 16, 128), F32)
@@ -372,7 +372,6 @@
     ggather = Gather(pc, gfull)
     ggather.first()
     received(lefts)
-    ggather.second()
     wscatter, wgather = [], []
     for q in range(2):
         for i in range(2):
@@ -380,6 +379,8 @@
             part = dot(lt, blend[...].reshape(512, 1024), 0, 0, HIGH)
             wbuf[q, 2 * i:2 * i + 2] = part.reshape(2, 4, 2, 8, 1024)
         wscatter.append(Scatter(pc, wbuf.at[q], wr1.at[q], wacc.at[q], wr2.at[q]))
+        if q == 0:
+            ggather.second()
         wscatter[q].first()
         wgather.append(Gather(pc, wall.at[q]))
     pc.drain(keep=18)
@@ -439,7 +440,7 @@
 
         return job
 
-    events = {(0, 18): w_step1, (1, 4): w_step2, (1, 20): w_step3, (2, 6): w_step4, (3, 12): w_last}
+    events = {(0, 28): w_step1, (1, 8): w_step2, (1, 20): w_step3, (2, 4): w_step4, (3, 12): w_last}
     flat = gfull[...].reshape(1280, 128)
     for b in range(10):
         work[b] = flat[128 * b:128 * b + 128]

time: 128 us -> 128 us (level)
  no operation moved by 1% of the time
where the time goes in v12:
time: 128 us
  Pallas kernels  127 us (99%)
    pallas_call x1, Pallas kernels, shards(): pl.pallas_call(kernel, out_shape=out_shape, in_specs=[anywhere, anywhere,...  124 us
    pallas_call x1, Pallas kernels, shards(): pl.pallas_call(place_kernel, out_shape=out_shape, in_specs=[anywhere] * 3...  2.93 us

profile of v12, /device:TPU:1, one launch (start us, length us, event | category | flops | bytes accessed | tf_op | source)
XLA Modules:
  0.0 127.8 jit_solution(9922913369779370061)
XLA Ops:
  0.6 124.0 %dion.1 = (bf16[2,256,1024]{2,1,0:T(8,128)(2,1)}, f32[2,256,1024]{2,1,0:T(8,128)}, f32[2,16,1024]{2,1,0:T(8,128)}) custom-call(bf16[2,256,1024]{2,1,0:T(8,128)(2,1)} %grad.1, f32[2,256,1024]{2,1,0:T(8,128)} %mom.1, f32[2,16,1024]{2,1,0:T(8,128)} %rb.1), custom_call_target="tpu_custom_call" | custom-call | tf_op jit(solution)/shard_map/dion/pallas_call | solution.py:617
  124.7 2.9 %place.1 = (bf16[2,256,1024]{2,1,0:T(8,128)(2,1)}, f32[2,256,1024]{2,1,0:T(8,128)}, f32[2,16,1024]{2,1,0:T(8,128)}) custom-call(bf16[2,256,1024]{2,1,0:T(8,128)(2,1)} %get-tuple-element.6.update, f32[2,256,1024]{2,1,0:T(8,128)} %get-tuple-element.7.momentum_next, f32[2,16,1024]{2,1,0:T(8,128)} %get-tuple-element.8.basis_next), custom_call_target="tpu_custom_call" | custom-call | tf_op jit(solution)/shard_map/place/pallas_call | solution.py:640
